TPU v7x, 32 devices: a whole 2x2x4 slice. The times are simulated.
32 devices in a mesh: groups: 2 (over x), replica: 8 (over z, y), tensor: 2 (over core).
Axes of the slice: x: 2, y: 2, z: 4, core: 2. Of those that a mesh axis runs over, the one named last changes fastest.
Arguments:
- tokens: bfloat16 [6144, 8192], P(('groups', 'replica')), parts along dimension 0, may hold values from -6 to 6
- queries: bfloat16 [6144, 4096], P(('groups', 'replica'), 'tensor'), parts along dimension 0, may hold values from -56 to 56
- stored_key_cache: bfloat16 [64, 2048, 512], P(('groups', 'replica'), None, 'tensor'), parts along dimension 0, may hold values from -6 to 6
- stored_value_cache: bfloat16 [64, 2048, 512], P(('groups', 'replica'), None, 'tensor'), parts along dimension 0, may hold values from -6 to 6
- key_weight_matrix: bfloat16 [8192, 512], P(None, 'tensor'), may hold values from -0.0625 to 0.0625
- value_weight_matrix: bfloat16 [8192, 512], P(None, 'tensor'), may hold values from -0.0625 to 0.0625
- adapter_down_weight: bfloat16 [16, 8192, 128], P('replica', 'tensor'), may hold values from -0.0625 to 0.0625
- adapter_up_weight: bfloat16 [16, 2, 64, 512], P('replica', None, None, 'tensor'), may hold values from -0.75 to 0.75
- adapter_slot_index: int32 [32], P('groups'), parts along dimension 0, may hold values from 0 to 15, as said below
- request_adapter_index: int32 [16, 4], P('groups'), parts along dimension 0, may hold values from 0 to 15, as said below
- fresh_token_count: int32 [16, 4], P(('groups', 'replica')), parts along dimension 0, may hold values from 1 to 128, 384 in all within a row
- cache_token_length: int32 [16, 4], P(('groups', 'replica')), parts along dimension 0, may hold values from 256 to 2048, as said below
Outputs:
- context: bfloat16 [6144, 4096], P(('groups', 'replica'), 'tensor'), parts along dimension 0
- new_keys: bfloat16 [6144, 512], P(('groups', 'replica'), 'tensor'), parts along dimension 0
- new_values: bfloat16 [6144, 512], P(('groups', 'replica'), 'tensor'), parts along dimension 0
There are 2 independent parts, one for each index of `groups`. A program takes and returns all parts, laid end to end along the dimension named above; an argument that names none is the same for every part. Nothing has to cross between parts.
Inputs may be any that keep to these rules, and one draw needn't show every extreme that they name: `adapter_slot_index`: a permutation: each slot holds one adapter. `request_adapter_index`: the 4 requests of one replica use adapters whose slots lie on 4 different replicas (slot // 2). `fresh_token_count`: the counts of one replica sum to 384. `cache_token_length`: some request holds exactly 2048 cached tokens.
All inputs are finite; a program needn't handle non-finite values.
Results may differ from a plain program's by a relative error of at most 0.0089.
Values may be sent and summed in bfloat16 or wider, within the bound.
No kernel may reach another device: no remote copies, remote signals or barrier semaphores. Data moves between devices by JAX's collectives and lax.ppermute only.
A program may use at most 320 MiB of HBM per device.

v0:
```python
import functools

import jax
import jax.numpy as jnp
import numpy as np
from jax import lax
from jax.experimental import pallas as pl
from jax.experimental.pallas import tpu as pltpu
from jax.sharding import PartitionSpec as P

HEAD = 128
GROUP = 8
RANK = 64
REQ = 4
SCALE = 0.5
THETA = 500000.0
LOG2E = 1.4426950408889634
NEG = -1e30
TILE = 32
CHUNK = 512
PART = 8
ALIGN = 16
VMEM = 60 * 1024 * 1024


def params(*sem, vmem=VMEM):
    return pltpu.CompilerParams(
        dimension_semantics=sem if sem else None, vmem_limit_bytes=vmem
    )


def nt_dot(a, b):
    return lax.dot_general(a, b, (((1,), (1,)), ((), ())), preferred_element_type=jnp.float32)


def cached_kernel(info, q_ref, k_ref, v_ref, *rest):
    acc_ref, stat_ref = rest[-2:]
    r = pl.program_id(0)
    rows_all = q_ref.shape[0]
    start = info[0, r]
    count = info[1, r]
    length = info[3, r]
    base0 = (start // ALIGN) * ALIGN
    tiles = (start + count - base0 + TILE - 1) // TILE
    units = (length + CHUNK - 1) // CHUNK
    factor = HEAD**-0.5 * LOG2E
    row_iota = lax.broadcasted_iota(jnp.int32, (TILE, 128), 0)
    lane = lax.broadcasted_iota(jnp.int32, (TILE, 128), 1)
    many = TILE * PART

    def tile(width, t, carry):
        base = pl.multiple_of(jnp.minimum(base0 + t * TILE, rows_all - TILE), ALIGN)
        qt = q_ref[pl.ds(base, TILE), :]
        q = jnp.concatenate([qt[:, h * HEAD : (h + 1) * HEAD] for h in range(PART)], axis=0)
        lanes = [slice(i * 128, (i + 1) * 128) for i in range(width // 128)]
        key_iota = lax.broadcasted_iota(jnp.int32, (1, width), 1)
        s = nt_dot(q, k_ref[0, :width, :]) + jnp.where(key_iota < length, 0.0, NEG)
        most = s[:, lanes[0]]
        for cut in lanes[1:]:
            most = jnp.maximum(most, s[:, cut])
        m = jnp.broadcast_to(jnp.max(most, axis=1, keepdims=True), (many, 128)) * factor
        l = jnp.zeros((many, 128), jnp.float32)
        weights = []
        for cut in lanes:
            p = jnp.exp2(s[:, cut] * factor - m)
            l = l + p
            weights.append(p.astype(jnp.bfloat16))
        acc = jnp.dot(
            jnp.concatenate(weights, axis=1),
            v_ref[0, :width, :],
            preferred_element_type=jnp.float32,
        )
        l = jnp.sum(l, axis=1, keepdims=True)
        at_row = row_iota + base
        mine = (at_row >= start) & (at_row < start + count)
        rows = pl.ds(base, TILE)
        tops = stat_ref[0, 0, rows, :]
        sums = stat_ref[0, 1, rows, :]
        for h in range(PART):
            part = slice(h * TILE, (h + 1) * TILE)
            columns = slice(h * HEAD, (h + 1) * HEAD)
            acc_ref[0, rows, columns] = jnp.where(mine, acc[part], acc_ref[0, rows, columns])
            here = mine & (lane == h)
            tops = jnp.where(here, m[part], tops)
            sums = jnp.where(here, l[part], sums)
        stat_ref[0, 0, rows, :] = tops
        stat_ref[0, 1, rows, :] = sums
        return carry

    for n in range(1, k_ref.shape[1] // CHUNK + 1):

        @pl.when(units == n)
        def _():
            lax.fori_loop(0, tiles, functools.partial(tile, n * CHUNK), 0)


def cached_attention(info, queries, cache_key, cache_value, part, before):
    rows = queries.shape[0]
    wide = PART * HEAD
    parts = queries.shape[1] // wide
    head = part * PART // GROUP
    slots = cache_key.shape[1]
    extra = [] if before is None else list(before)
    acc_spec = pl.BlockSpec((1, rows, wide), lambda r, s: (part, 0, 0))
    stat_spec = pl.BlockSpec((1, 2, rows, 128), lambda r, s: (part, 0, 0, 0))
    cache = pl.BlockSpec((1, slots, HEAD), lambda r, s: (r, 0, head))
    return pl.pallas_call(
        cached_kernel,
        grid_spec=pltpu.PrefetchScalarGridSpec(
            num_scalar_prefetch=1,
            grid=(REQ,),
            in_specs=[pl.BlockSpec((rows, wide), lambda r, s: (0, part)), cache, cache]
            + [pl.BlockSpec(memory_space=pltpu.HBM)] * len(extra),
            out_specs=[acc_spec, stat_spec],
        ),
        out_shape=[
            jax.ShapeDtypeStruct((parts, rows, wide), jnp.float32),
            jax.ShapeDtypeStruct((parts, 2, rows, 128), jnp.float32),
        ],
        input_output_aliases={4: 0, 5: 1} if extra else {},
        compiler_params=params("arbitrary"),
        cost_estimate=pl.CostEstimate(
            flops=4 * rows * wide * 4096,
            bytes_accessed=6 * 1024 * 1024,
            transcendentals=rows * PART * 2048,
        ),
        name="cached_attention",
    )(info, queries, cache_key, cache_value, *extra)


def low_rank_kernel(pick, n_pieces, place, infos, *refs):
    tokens = refs[:4]
    pieces = refs[4 : 4 + n_pieces]
    before = refs[4 + n_pieces : -3]
    outs = refs[-3 - (8 if pick == "early" else 4) : -3]
    token_scr, piece_scr, sems = refs[-3:]
    rows, width = token_scr.shape[1:]
    held = piece_scr.shape[1]
    column = pl.multiple_of(place[2] * width, 128)
    copies = [
        pltpu.make_async_copy(tokens[0].at[:, pl.ds(column, width)], token_scr.at[0], sems.at[0])
    ]
    for n in range(1, 4):
        copies.append(
            pltpu.make_async_copy(tokens[n].at[pl.ds(0, rows)], token_scr.at[n], sems.at[n])
        )
    at = 0
    for p in range(n_pieces):
        if len(pieces[p].shape) == 4:
            target = piece_scr.at[pl.ds(at, pieces[p].shape[0])]
            at += pieces[p].shape[0]
        else:
            target = piece_scr.at[at]
            at += 1
        copies.append(pltpu.make_async_copy(pieces[p], target, sems.at[4 + p]))
    for copy in copies:
        copy.start()
    for n in range(4):
        outs[n][...] = jnp.zeros_like(outs[n]) if pick == "early" else before[n][...]
    for copy in copies:
        copy.wait()
    window = rows // 3 + ALIGN
    row_iota = lax.broadcasted_iota(jnp.int32, (window, 1), 0)
    z, y = place[0], place[1]
    at_end = (z == 0) | (z == 3)

    for n in range(4):

        def one(r, start):
            count = infos[n, r]
            slot = infos[n, REQ + r]
            owner = slot // held
            layer = owner // 2
            other = jnp.where(owner % 2 != y, 1, 0)
            mates = layer // 2 == z // 2
            ends = (layer == 0) | (layer == 3)
            last = at_end & ends & jnp.logical_not(mates)
            if pick == "early":
                kind = jnp.where(at_end, 4, jnp.where(ends, 3, 2))
                kind = jnp.where(mates, jnp.where(layer == z, 0, 1), kind)
                index = kind * 2 + other
                valid = jnp.logical_not(last)
            else:
                index = other
                valid = last

            def product():
                base = pl.multiple_of(
                    jnp.minimum((start // ALIGN) * ALIGN, rows - window), ALIGN
                )
                span = pl.ds(base, window)
                low = jnp.dot(
                    token_scr[n, span, :],
                    piece_scr[index, slot % held, :width, :],
                    preferred_element_type=jnp.float32,
                )
                mine = (row_iota + base >= start) & (row_iota + base < start + count) & valid
                outs[n][span, :] = jnp.where(mine, low, outs[n][span, :])

            if pick == "early":
                product()
                outs[4 + n][r] = jnp.where(
                    last,
                    before[0][other, slot % held],
                    piece_scr[index, slot % held, width:, :],
                )
            else:
                pl.when(valid)(product)
            return start + count

        if pick == "early":
            start = jnp.int32(0)
            for r in range(REQ):
                start = one(r, start)
        else:
            lax.fori_loop(0, REQ, one, 0)


def low_rank_step(pick, place, infos, tokens, pieces, before, width):
    rows = tokens[0].shape[0]
    held, tall, rank = pieces[0].shape[-3:]
    vmem = pl.BlockSpec(memory_space=pltpu.VMEM)
    smem = pl.BlockSpec(memory_space=pltpu.SMEM)
    hbm = pl.BlockSpec(memory_space=pltpu.HBM)
    total = sum(p.shape[0] if p.ndim == 4 else 1 for p in pieces)
    ups = []
    if pick == "early":
        ups = [jax.ShapeDtypeStruct((REQ, tall - width, rank), jnp.bfloat16)] * 4
    return pl.pallas_call(
        functools.partial(low_rank_kernel, pick, len(pieces)),
        in_specs=[smem, smem] + [hbm] * (4 + len(pieces)) + [vmem] * len(before),
        out_specs=[vmem] * (4 + len(ups)),
        out_shape=[jax.ShapeDtypeStruct((rows, rank), jnp.float32)] * 4 + ups,
        scratch_shapes=[
            pltpu.VMEM((4, rows, width), jnp.bfloat16),
            pltpu.VMEM((total, held, tall, rank), jnp.bfloat16),
            pltpu.SemaphoreType.DMA((4 + len(pieces),)),
        ],
        compiler_params=params(),
        cost_estimate=pl.CostEstimate(
            flops=2 * 4 * rows * width * rank * 4, bytes_accessed=6 * 1024 * 1024, transcendentals=0
        ),
        name="low_rank_" + pick,
    )(place, infos, *tokens, *pieces, *before)


def final_kernel(
    info, mine_ref, other_ref, pk_ref, pv_ref, up0, up1, up2, up3, cos_ref, sin_ref, q_ref, acc_ref,
    stat_ref, ctx_ref, ko_ref, vo_ref, up_scr,
):
    rows = q_ref.shape[0]

    @pl.when(pl.program_id(0) % (GROUP // PART) == 0)
    def _():
        low = (mine_ref[...] + other_ref[...]).astype(jnp.bfloat16)
        at_row = lax.broadcasted_iota(jnp.int32, (rows, 1), 0)
        key_lin = pk_ref[...]
        value_lin = pv_ref[...]
        for n, ref in enumerate((up0, up1, up2, up3)):
            up_scr[n] = ref[...]
        tall = RANK // 2
        which = pl.ds(
            pl.multiple_of(pl.program_id(0) // (GROUP // PART) * tall, tall), tall
        )
        for r in range(REQ):
            mine = (at_row >= info[0, r]) & (at_row < info[0, r] + info[1, r])
            up = [up_scr[info[2, c], r, which, :] for c in range(4)]
            up_key = jnp.concatenate(up[:2], axis=0)
            up_value = jnp.concatenate(up[2:], axis=0)
            dk = jnp.dot(low[:, :RANK], up_key, preferred_element_type=jnp.float32)
            dv = jnp.dot(low[:, RANK:], up_value, preferred_element_type=jnp.float32)
            key_lin = key_lin + SCALE * jnp.where(mine, dk, 0.0)
            value_lin = value_lin + SCALE * jnp.where(mine, dv, 0.0)
        turned = key_lin * cos_ref[...] + pltpu.roll(key_lin, HEAD // 2, 1) * sin_ref[...]
        ko_ref[...] = turned.astype(jnp.bfloat16)
        vo_ref[...] = value_lin.astype(jnp.bfloat16)

    factor = HEAD**-0.5 * LOG2E
    most = rows // 3
    span = 2 * most

    def block(b, carry):
        low_key = pl.multiple_of(jnp.maximum(b - 1, 0) * most, most)
        at = pl.multiple_of(b * most, most)
        q_at = lax.broadcasted_iota(jnp.int32, (most, 1), 0) + at
        k_at = lax.broadcasted_iota(jnp.int32, (1, span), 1) + low_key
        q_req = jnp.zeros((most, 1), jnp.int32)
        k_req = jnp.zeros((1, span), jnp.int32)
        for r in range(1, REQ):
            q_req = q_req + (q_at >= info[0, r]).astype(jnp.int32)
            k_req = k_req + (k_at >= info[0, r]).astype(jnp.int32)
        bias = jnp.where((q_req == k_req) & (k_at <= q_at), 0.0, NEG)
        part = pl.ds(at, most)
        lane = lax.broadcasted_iota(jnp.int32, (most, 128), 1)
        heads = [slice(h * HEAD, (h + 1) * HEAD) for h in range(PART)]
        cuts = [slice(h * most, (h + 1) * most) for h in range(PART)]
        q = jnp.concatenate([q_ref[part, h] for h in heads], axis=0)
        scores = nt_dot(q, ko_ref[pl.ds(low_key, span), :])
        fresh_top = jnp.zeros((most, 128), jnp.float32)
        fresh_sum = jnp.ones((most, 128), jnp.float32)
        weights = []
        for h in range(PART):
            s = scores[cuts[h]] * factor + bias
            top = jnp.max(s, axis=1, keepdims=True)
            p = jnp.exp2(s - top)
            fresh_top = jnp.where(lane == h, top, fresh_top)
            fresh_sum = jnp.where(lane == h, jnp.sum(p, axis=1, keepdims=True), fresh_sum)
            weights.append(p.astype(jnp.bfloat16))
        fresh = jnp.dot(
            jnp.concatenate(weights, axis=0),
            vo_ref[pl.ds(low_key, span), :],
            preferred_element_type=jnp.float32,
        )
        live = lane < PART
        before = jnp.where(live, stat_ref[0, 0, part, :], 0.0)
        before_sum = jnp.where(live, stat_ref[0, 1, part, :], 1.0)
        top = jnp.maximum(before, fresh_top)
        old = jnp.exp2(before - top)
        new = jnp.exp2(fresh_top - top)
        total = before_sum * old + fresh_sum * new
        old = old / total
        new = new / total
        for h in range(PART):
            out = (
                acc_ref[0, part, heads[h]] * old[:, h : h + 1]
                + fresh[cuts[h]] * new[:, h : h + 1]
            )
            ctx_ref[part, heads[h]] = out.astype(jnp.bfloat16)
        return carry

    lax.fori_loop(0, 3, block, 0)


def final_step(info, mine, other, pk, pv, ups, cosine, sine, queries, acc, stat):
    rows = queries.shape[0]
    wide = PART * HEAD
    parts = queries.shape[1] // wide
    each = GROUP // PART
    heads = parts // each
    rank2 = mine.shape[1]
    whole = lambda shape: pl.BlockSpec(shape, lambda i, s: (0,) * len(shape))
    of_head = pl.BlockSpec((rows, HEAD), lambda i, s: (0, i // each))
    return pl.pallas_call(
        final_kernel,
        grid_spec=pltpu.PrefetchScalarGridSpec(
            num_scalar_prefetch=1,
            grid=(parts,),
            in_specs=[
                whole((rows, rank2)),
                whole((rows, rank2)),
                of_head,
                of_head,
                *([whole(ups[0].shape)] * 4),
                whole((rows, HEAD)),
                whole((rows, HEAD)),
                pl.BlockSpec((rows, wide), lambda i, s: (0, i)),
                pl.BlockSpec((1, rows, wide), lambda i, s: (i, 0, 0)),
                pl.BlockSpec((1, 2, rows, 128), lambda i, s: (i, 0, 0, 0)),
            ],
            out_specs=[pl.BlockSpec((rows, wide), lambda i, s: (0, i)), of_head, of_head],
            scratch_shapes=[pltpu.VMEM((4, *ups[0].shape), jnp.bfloat16)],
        ),
        out_shape=[
            jax.ShapeDtypeStruct(queries.shape, jnp.bfloat16),
            jax.ShapeDtypeStruct((rows, heads * HEAD), jnp.bfloat16),
            jax.ShapeDtypeStruct((rows, heads * HEAD), jnp.bfloat16),
        ],
        compiler_params=params("arbitrary", vmem=VMEM // 2),
        name="final_step",
    )(info, mine, other, pk, pv, *ups, cosine, sine, queries, acc, stat)


def after(value, *others):
    return lax.optimization_barrier((value, *others))[0]


def body(
    fast,
    tokens,
    queries,
    stored_key_cache,
    stored_value_cache,
    key_weight_matrix,
    value_weight_matrix,
    adapter_down_weight,
    adapter_up_weight,
    adapter_slot_index,
    request_adapter_index,
    fresh_token_count,
    cache_token_length,
):
    group = lax.axis_index("groups")
    replica = lax.axis_index("replica")
    core = lax.axis_index("tensor")
    rows, width = tokens.shape
    held, half, rank2 = adapter_down_weight.shape
    counts = fresh_token_count[0]
    lengths = cache_token_length[0]
    order = jnp.arange(REQ, dtype=jnp.int32)
    starts = jnp.sum(jnp.where(order[:, None] > order[None, :], counts[None, :], 0), axis=1)
    wanted = lax.dynamic_index_in_dim(request_adapter_index, replica, 0, False)
    n_slots = adapter_slot_index.shape[0]
    slots = jnp.sum(
        jnp.where(
            wanted[:, None] == jnp.arange(n_slots, dtype=jnp.int32)[None, :],
            adapter_slot_index[None, :],
            0,
        ),
        axis=1,
    )
    here = group * 2 + replica % 2 if fast else 0
    info = jnp.stack([starts, counts, order ^ here, lengths]).astype(jnp.int32)

    at_row = jnp.arange(rows, dtype=jnp.int32)
    of_request = jnp.sum(at_row[:, None] >= starts[None, 1:], axis=1)
    shift = lengths - starts
    position = at_row + jnp.sum(
        jnp.where(of_request[:, None] == jnp.arange(REQ)[None, :], shift[None, :], 0), axis=1
    )
    frequency = THETA ** (-(jnp.arange(HEAD // 2, dtype=jnp.float32) * 2.0) / HEAD)
    angles = position.astype(jnp.float32)[:, None] * frequency
    cosine = jnp.cos(angles)
    sine = jnp.sin(angles)
    cosine = jnp.concatenate([cosine, cosine], axis=1)
    sine = jnp.concatenate([-sine, sine], axis=1)

    n_replica = lax.axis_size("replica")
    tall = RANK // 2

    if fast:
        y = replica % 2
        column = group * 2 + y
        quarter = half // 4
        by_x = lambda a: lax.ppermute(a, "groups", [(0, 1), (1, 0)])
        by_y = lambda a: lax.ppermute(a, "replica", [(r, r ^ 1) for r in range(n_replica)])
        by_xy = lambda a: lax.ppermute(
            a,
            ("groups", "replica"),
            [
                (g * n_replica + r, (1 - g) * n_replica + (r ^ 1))
                for g in range(2)
                for r in range(n_replica)
            ],
        )
        mesh_z = lambda a, pairs: lax.ppermute(
            a, "replica", [(2 * f + p, 2 * t + p) for f, t in pairs for p in range(2)]
        )
        in_pair = lambda a: mesh_z(a, [(0, 1), (1, 0), (2, 3), (3, 2)])
        across = lambda a: mesh_z(a, [(1, 2), (2, 1)])
        outward = lambda a: mesh_z(a, [(1, 0), (2, 3)])

        def factor_part(c, factors):
            down = lax.dynamic_slice_in_dim(factors, c * quarter, quarter, 1)
            up = lax.dynamic_slice(
                adapter_up_weight,
                (0, c // 2, (c % 2) * tall, 0),
                (held, 1, tall, adapter_up_weight.shape[3]),
            )[:, 0]
            return jnp.concatenate([down, up[:, :, :HEAD], up[:, :, HEAD:]], axis=1)

        to_mate = factor_part(column ^ 1, adapter_down_weight)
        own_b = by_y(to_mate)
        own_a = factor_part(column, after(adapter_down_weight, to_mate))
        pair_a = in_pair(own_a)
        mid_a = across(own_a)
        note = jnp.concatenate([counts, slots])
        below = jnp.pad(note.astype(jnp.bfloat16)[None, :], ((0, 15), (0, quarter - 2 * REQ)))
        token_part = lambda c: jnp.concatenate(
            [lax.dynamic_slice_in_dim(tokens, core * half + c * quarter, quarter, 1), below]
        )
        for_x, for_y, for_d = (token_part(column ^ c) for c in (2, 1, 3))
        t_x = by_x(for_x)
        own_b, for_y, for_d = lax.optimization_barrier((own_b, for_y, for_d))
        t_y = by_y(for_y)
        t_d = by_xy(for_d)
        tokens_later = after(tokens, own_b)
        far_up = mesh_z(jnp.stack([own_a[:, quarter:], own_b[:, quarter:]]), [(0, 3), (3, 0)])
        pair_b = in_pair(own_b)
        mid_b = across(own_b)
        plain_key = jnp.dot(tokens_later, key_weight_matrix, preferred_element_type=jnp.float32)
        part = lambda n, q, b: cached_attention(
            info, q, stored_key_cache, stored_value_cache, n, b
        )
        across_2 = across(after(jnp.stack([pair_a, pair_b]), plain_key))
        outward_2 = outward(after(jnp.stack([mid_a, mid_b]), plain_key))
        cached = part(0, after(queries, pair_b, mid_b, far_up, t_x, plain_key), None)
        outward_3 = outward(after(across_2, cached[0]))
        plain_value = jnp.dot(
            after(tokens, cached[0]), value_weight_matrix, preferred_element_type=jnp.float32
        )
        place = jnp.stack([replica // 2, y, core * 4 + column]).astype(jnp.int32)
        t_y, t_x, t_d, _ = lax.optimization_barrier((t_y, t_x, t_d, plain_value))
        infos = jnp.stack(
            [note] + [t[rows, : 2 * REQ].astype(jnp.int32) for t in (t_y, t_x, t_d)]
        )
        layer_tokens = [tokens, t_y, t_x, t_d]
        early = [own_a, own_b, pair_a, pair_b, mid_a, mid_b, across_2, outward_2]
        low = low_rank_step("early", place, infos, layer_tokens, early, [far_up], quarter)
        ups = [low[4], by_y(low[5]), by_x(low[6]), by_xy(low[7])]
        cached = part(1, after(queries, low[0]), cached)
        outward_3 = after(outward_3, cached[0], *ups)
        low = low_rank_step("late", place, infos, layer_tokens, [outward_3], low[:4], quarter)
        low_sum = low[0] + by_y(low[1]) + by_x(low[2]) + by_xy(low[3])
    else:
        down_all = lax.all_gather(adapter_down_weight, "replica", axis=0, tiled=True)
        mine = lax.dynamic_slice_in_dim(tokens, core * half, half, 1)
        low_sum = jnp.zeros((rows, rank2), jnp.float32)
        for r in range(REQ):
            low_sum = low_sum + jnp.where(
                (of_request == r)[:, None],
                jnp.dot(mine, down_all[slots[r]], preferred_element_type=jnp.float32),
                0.0,
            )
        up_all = lax.all_gather(adapter_up_weight, "replica", axis=0, tiled=True)[slots]
        ups = []
        for c in range(4):
            up = up_all[:, c // 2, (c % 2) * tall : (c % 2 + 1) * tall]
            ups.append(jnp.concatenate([up[:, :, :HEAD], up[:, :, HEAD:]], axis=1))
        plain_key = jnp.dot(tokens, key_weight_matrix, preferred_element_type=jnp.float32)
        plain_value = jnp.dot(tokens, value_weight_matrix, preferred_element_type=jnp.float32)
        cached = None
        for n in range(queries.shape[1] // (PART * HEAD)):
            cached = cached_attention(
                info, queries, stored_key_cache, stored_value_cache, n, cached
            )
    low_other = lax.ppermute(low_sum, "tensor", [(0, 1), (1, 0)])
    return tuple(
        final_step(
            info, low_sum, low_other, plain_key, plain_value, ups, cosine, sine, queries, *cached
        )
    )


def layered(mesh):
    return dict(mesh.shape) == {"groups": 2, "replica": 8, "tensor": 2}


def solution(mesh):
    rows = P(("groups", "replica"), None)
    split = P(("groups", "replica"), "tensor")
    cache = P(("groups", "replica"), None, "tensor")
    placed = (
        rows,
        split,
        cache,
        cache,
        P(None, "tensor"),
        P(None, "tensor"),
        P("replica", "tensor", None),
        P("replica", None, None, "tensor"),
        P("groups"),
        P("groups", None),
        rows,
        rows,
    )
    return jax.shard_map(
        functools.partial(body, layered(mesh)),
        mesh=mesh,
        in_specs=placed,
        out_specs=(split, split, split),
        check_vma=False,
    )
```

profile of v0, /device:TPU:9, one launch (start us, length us, event | category | flops | bytes accessed | tf_op | source)
XLA Modules:
  0.0 130.1 jit_solution(11271243340899105985)
XLA Ops:
  0.7 1.5 %copy-done = bf16[2,4096,128]{2,1,0:T(8,128)(2,1)S(1)} copy-done((bf16[2,4096,128]{2,1,0:T(8,128)(2,1)S(1)}, bf16[2,4096,128]{2,1,0:T(8,128)(2,1)}, u32[]{:S(2)}) %copy-start) | copy-done | bytes 2097176
  4.0 1.2 collective-permute-start
  5.3 0.9 pad_maximum_fusion.6.refs_4_
  6.1 3.2 %collective-permute-start.10 = (bf16[2,1088,128]{2,1,0:T(8,128)(2,1)}, bf16[2,1088,128]{2,1,0:T(8,128)(2,1)}, u32[]{:S(2)}, u32[]{:S(2)}) collective-permute-start(bf16[2,1088,128]{2,1,0:T(8,128)(2,1)} %pad_maximum_fusion.6.refs_4_), channel_id=1, source_target_pairs={{4,8},{6,10},{8,4},{10,6},{5,9},{7,11},{9,5},{11,7},{20,24},{22,26... | collective-permute-start | bytes 1671176 | tf_op jit(solution)/shard_map/ppermute | solution.py:445
  9.9 1.8 %constant_dynamic-slice_fusion.1 = (bf16[384,1024]{1,0:T(8,128)(2,1)S(1)}, bf16[384,1024]{1,0:T(8,128)(2,1)S(1)}, bf16[384,1024]{1,0:T(8,128)(2,1)S(1)}) fusion(bf16[384,8192]{1,0:T(8,128)(2,1)} %refs_0_.3, s32[]{:T(128)S(6)} %select_n.82, s32[]{:T(128)S(6)} %select_n.81, s32[]{:T(128)S(6)} %select_n.80), kind=kLoop, calls=%fused_computation.38 | loop fusion | bytes 4718604 | tf_op jit(solution)/shard_map/dynamic_slice | solution.py:469
  11.8 1.5 %pad_maximum_fusion = (bf16[400,1024]{1,0:T(8,128)(2,1)}, bf16[400,1024]{1,0:T(8,128)(2,1)}, bf16[400,1024]{1,0:T(8,128)(2,1)}) fusion(bf16[16,1024]{1,0:T(8,128)(2,1)S(1)} %fusion.6, bf16[384,1024]{1,0:T(8,128)(2,1)S(1)} %get-tuple-element.65, bf16[384,1024]{1,0:T(8,128)(2,1)S(1)} %get-tuple-element.66, bf16[384,1024]{1,0:T(8,128)(2,1)S(1)} %get-tuple-element.67), kind=kLoop, calls=%fused_computation | loop fusion | flops 4096000 | bytes 4849664 | tf_op jit(solution)/shard_map/concatenate | solution.py:468
  13.3 1.2 collective-permute-start.2
  16.0 1.8 %collective-permute-done.refs_5_ = bf16[2,1088,128]{2,1,0:T(8,128)(2,1)} collective-permute-done((bf16[2,1088,128]{2,1,0:T(8,128)(2,1)}, bf16[2,1088,128]{2,1,0:T(8,128)(2,1)}, u32[]{:S(2)}, u32[]{:S(2)}) %collective-permute-start) | collective-permute-done | bytes 557088 | tf_op jit(solution)/shard_map/ppermute | solution.py:435
  17.8 3.2 %collective-permute-start.5 = (bf16[2,1088,128]{2,1,0:T(8,128)(2,1)}, bf16[2,1088,128]{2,1,0:T(8,128)(2,1)S(1)}, u32[]{:S(2)}, u32[]{:S(2)}) collective-permute-start(bf16[2,1088,128]{2,1,0:T(8,128)(2,1)} %collective-permute-done.refs_5_), channel_id=1, source_target_pairs={{4,8},{6,10},{8,4},{10,6},{5,9},{7,11},{9,5},{11,7},{20,24},{22,26... | collective-permute-start | bytes 1671176 | tf_op jit(solution)/shard_map/ppermute | solution.py:445
  21.1 5.8 %fusion.9.pk_ref = f32[384,256]{1,0:T(8,128)S(1)} fusion(bf16[384,8192]{1,0:T(8,128)(2,1)} %refs_0_.3, bf16[8192,256]{1,0:T(8,128)(2,1)} %param.16), kind=kOutput, calls=%fused_computation.54 | convolution fusion | flops 1610612736 | bytes 10878976 | tf_op jit(solution)/shard_map/dot_general | solution.py:480
  28.3 4.7 %collective-permute-done.5.refs_9_ = bf16[2,1088,128]{2,1,0:T(8,128)(2,1)S(1)} collective-permute-done((bf16[2,1088,128]{2,1,0:T(8,128)(2,1)}, bf16[2,1088,128]{2,1,0:T(8,128)(2,1)S(1)}, u32[]{:S(2)}, u32[]{:S(2)}) %collective-permute-start.5) | collective-permute-done | bytes 557088 | tf_op jit(solution)/shard_map/ppermute | solution.py:445
  33.7 2.2 %pad_maximum_fusion.4 = bf16[2,2,1088,128]{3,2,1,0:T(8,128)(2,1)} fusion(bf16[1,2,1088,128]{3,2,1,0:T(8,128)(2,1)S(1)} %bitcast.28, bf16[1,2,1088,128]{3,2,1,0:T(8,128)(2,1)} %bitcast.13), kind=kLoop, calls=%fused_computation.4 | loop fusion | flops 557056 | bytes 2228224 | tf_op jit(solution)/shard_map/stack | solution.py:485
  35.9 1.7 %collective-permute-start.3 = (bf16[400,1024]{1,0:T(8,128)(2,1)}, bf16[400,1024]{1,0:T(8,128)(2,1)}, u32[]{:S(2)}, u32[]{:S(2)}) collective-permute-start(bf16[400,1024]{1,0:T(8,128)(2,1)} %get-tuple-element.35), channel_id=1, source_target_pairs={{0,18},{2,16},{4,22},{6,20},{8,26},{10,24},{12,30},{14,28},{16,2},... | collective-permute-start | bytes 2457608 | tf_op jit(solution)/shard_map/ppermute | solution.py:436
  37.6 2.3 %collective-permute-start.11 = (bf16[2,2,1088,128]{3,2,1,0:T(8,128)(2,1)}, bf16[2,2,1088,128]{3,2,1,0:T(8,128)(2,1)}, u32[]{:S(2)}, u32[]{:S(2)}) collective-permute-start(bf16[2,2,1088,128]{3,2,1,0:T(8,128)(2,1)} %pad_maximum_fusion.4), channel_id=1, source_target_pairs={{4,0},{6,2},{8,12},{10,14},{5,1},{7,3},{9,13},{11,15},{20,16},{22,... | collective-permute-start | bytes 3342344 | tf_op jit(solution)/shard_map/ppermute | solution.py:445
  39.9 2.1 %pad_maximum_fusion.3 = bf16[2,2,1088,128]{3,2,1,0:T(8,128)(2,1)} fusion(bf16[1,2,1088,128]{3,2,1,0:T(8,128)(2,1)S(1)} %bitcast.29, bf16[1,2,1088,128]{3,2,1,0:T(8,128)(2,1)} %bitcast.11), kind=kLoop, calls=%fused_computation.3 | loop fusion | flops 557056 | bytes 2228224 | tf_op jit(solution)/shard_map/stack | solution.py:484
  42.1 3.2 %collective-permute-start.8 = (bf16[2,2,1088,128]{3,2,1,0:T(8,128)(2,1)}, bf16[2,2,1088,128]{3,2,1,0:T(8,128)(2,1)}, u32[]{:S(2)}, u32[]{:S(2)}) collective-permute-start(bf16[2,2,1088,128]{3,2,1,0:T(8,128)(2,1)} %pad_maximum_fusion.3), channel_id=1, source_target_pairs={{4,8},{6,10},{8,4},{10,6},{5,9},{7,11},{9,5},{11,7},{20,24},{22,26... | collective-permute-start | bytes 3342344 | tf_op jit(solution)/shard_map/ppermute | solution.py:445
  45.3 15.5 %cached_attention.2 = (f32[2,384,1024]{2,1,0:T(8,128)}, f32[2,2,384,128]{3,2,1,0:T(8,128)}) custom-call(s32[4,4]{1,0:T(4,128)} %pad_add_fusion.info, bf16[384,2048]{1,0:T(8,128)(2,1)} %q_ref.3, bf16[4,2048,256]{2,1,0:T(8,128)(2,1)} %k_ref.3, bf16[4,2048,256]{2,1,0:T(8,128)(2,1)} %v_ref.3), custom_call_target="tpu_custom_call" | custom-call | flops 6442450944 | bytes 6291456 | tf_op jit(solution)/shard_map/cached_attention/pallas_call | solution.py:107
  60.8 5.8 %fusion.10.pv_ref = f32[384,256]{1,0:T(8,128)S(1)} fusion(bf16[384,8192]{1,0:T(8,128)(2,1)} %refs_0_.3, bf16[8192,256]{1,0:T(8,128)(2,1)} %param.17), kind=kOutput, calls=%fused_computation.55 | convolution fusion | flops 1610612736 | bytes 10878976 | tf_op jit(solution)/shard_map/dot_general | solution.py:488
  66.6 1.4 %collective-permute-done.1.refs_1_ = bf16[400,1024]{1,0:T(8,128)(2,1)} collective-permute-done((bf16[400,1024]{1,0:T(8,128)(2,1)}, bf16[400,1024]{1,0:T(8,128)(2,1)}, u32[]{:S(2)}, u32[]{:S(2)}) %collective-permute-start.1) | collective-permute-done | bytes 819232 | tf_op jit(solution)/shard_map/ppermute | solution.py:435
  68.7 2.3 %collective-permute-start.9 = (bf16[2,2,1088,128]{3,2,1,0:T(8,128)(2,1)}, bf16[2,2,1088,128]{3,2,1,0:T(8,128)(2,1)}, u32[]{:S(2)}, u32[]{:S(2)}) collective-permute-start(bf16[2,2,1088,128]{3,2,1,0:T(8,128)(2,1)} %collective-permute-done.8.refs_10_), channel_id=1, source_target_pairs={{4,0},{6,2},{8,12},{10,14},{5,1},{7,3},{9,13},{11,15},{20,16},{22,... | collective-permute-start | bytes 3342344 | tf_op jit(solution)/shard_map/ppermute | solution.py:445
  72.2 6.7 %low_rank_early.1 = (f32[384,128]{1,0:T(8,128)}, f32[384,128]{1,0:T(8,128)}, f32[384,128]{1,0:T(8,128)}, f32[384,128]{1,0:T(8,128)}, bf16[4,64,128]{2,1,0:T(8,12...) custom-call(s32[3]{0:T(128)} %pad_add_fusion.2.place, ...), custom_call_target="tpu_custom_call" | custom-call | flops 1610612736 | bytes 6291456 | tf_op jit(solution)/shard_map/low_rank_early/pallas_call | solution.py:229
  78.9 1.3 collective-permute-start.12
  80.2 1.2 collective-permute-start.13
  81.6 15.5 %cached_attention.3 = (f32[2,384,1024]{2,1,0:T(8,128)}, f32[2,2,384,128]{3,2,1,0:T(8,128)}) custom-call(s32[4,4]{1,0:T(4,128)} %pad_add_fusion.info, bf16[384,2048]{1,0:T(8,128)(2,1)} %q_ref.3, bf16[4,2048,256]{2,1,0:T(8,128)(2,1)} %k_ref.3, bf16[4,2048,256]{2,1,0:T(8,128)(2,1)} %v_ref.3, ...), custom_call_target="tpu_custom_call", output_to_operand_aliasing={{0}: (4, {}), {1}: (5, {})} | custom-call | flops 6442450944 | bytes 6291456 | tf_op jit(solution)/shard_map/cached_attention/pallas_call | solution.py:107
  97.1 4.4 %low_rank_late.1 = (f32[384,128]{1,0:T(8,128)}, f32[384,128]{1,0:T(8,128)}, f32[384,128]{1,0:T(8,128)}, f32[384,128]{1,0:T(8,128)}) custom-call(s32[3]{0:T(128)} %pad_add_fusion.2.place, s32[4,8]{1,0:T(4,128)} %pad_add_fusion.1.infos, bf16[384,8192]{1,0:T(8,128)(2,1)} %refs_0_.3, bf16[400,1024]{1,0:T(8,128)(2,1)} %collective-permute-done.1.refs_1_, ...), custom_call_target="tpu_custom_call" | custom-call | flops 1610612736 | bytes 6291456 | tf_op jit(solution)/shard_map/low_rank_late/pallas_call | solution.py:229
  102.4 3.2 %collective-permute-start.16 = (f32[384,128]{1,0:T(8,128)}, f32[384,128]{1,0:T(8,128)S(1)}, u32[]{:S(2)}, u32[]{:S(2)}) collective-permute-start(f32[384,128]{1,0:T(8,128)} %get-tuple-element.62), channel_id=1, source_target_pairs={{0,16},{16,0},{1,17},{17,1},{2,18},{18,2},{3,19},{19,3},{4,20},{20... | collective-permute-start | bytes 589832 | tf_op jit(solution)/shard_map/ppermute | solution.py:434
  106.3 2.5 %collective-permute-done.16 = f32[384,128]{1,0:T(8,128)S(1)} collective-permute-done((f32[384,128]{1,0:T(8,128)}, f32[384,128]{1,0:T(8,128)S(1)}, u32[]{:S(2)}, u32[]{:S(2)}) %collective-permute-start.16) | collective-permute-done | bytes 196640 | tf_op jit(solution)/shard_map/ppermute | solution.py:434
  108.9 2.5 %collective-permute-done.17 = f32[384,128]{1,0:T(8,128)S(1)} collective-permute-done((f32[384,128]{1,0:T(8,128)}, f32[384,128]{1,0:T(8,128)S(1)}, u32[]{:S(2)}, u32[]{:S(2)}) %collective-permute-start.17) | collective-permute-done | bytes 196640 | tf_op jit(solution)/shard_map/ppermute | solution.py:436
  111.4 1.0 add_add_fusion.mine_ref
  112.4 6.0 %collective-permute-start.18 = (f32[384,128]{1,0:T(8,128)S(1)}, f32[384,128]{1,0:T(8,128)S(1)}, u32[]{:S(2)}, u32[]{:S(2)}) collective-permute-start(f32[384,128]{1,0:T(8,128)S(1)} %add_add_fusion.mine_ref), channel_id=1, source_target_pairs={{0,1},{1,0},{2,3},{3,2},{4,5},{5,4},{6,7},{7,6},{8,9},{9,8},{10,11... | collective-permute-start | bytes 589832 | tf_op jit(solution)/shard_map/ppermute | solution.py:526
  119.5 1.9 %copy-done.1 = f32[2,384,1024]{2,1,0:T(8,128)S(1)} copy-done((f32[2,384,1024]{2,1,0:T(8,128)S(1)}, f32[2,384,1024]{2,1,0:T(8,128)}, u32[]{:S(2)}) %copy-start.1) | copy-done | bytes 3145752
  121.3 8.8 %final_step.1 = (bf16[384,2048]{1,0:T(8,128)(2,1)}, bf16[384,256]{1,0:T(8,128)(2,1)}, bf16[384,256]{1,0:T(8,128)(2,1)}) custom-call(s32[4,4]{1,0:T(4,128)S(1)} %copy-done.5, f32[384,128]{1,0:T(8,128)S(1)} %add_add_fusion.mine_ref, f32[384,128]{1,0:T(8,128)S(1)} %collective-permute-done.18.other_ref, f32[384,256]{1,0:T(8,128)S(1)} %fusion.9.pk_ref, ...), custom_call_target="tpu_custom_call" | custom-call | tf_op jit(solution)/shard_map/final_step/pallas_call | solution.py:343
  (77 shorter events, 10.8 us)
Async XLA Ops:
  3.1 6.3 %copy-start.10 = (s32[8,4]{0,1:T(4,128)S(1)}, s32[8,4]{0,1:T(4,128)}, u32[]{:S(2)}) copy-start(s32[8,4]{0,1:T(4,128)} %param.21) | copy-start | bytes 388
  3.1 6.5 %copy-start.13 = (s32[16]{0:T(128)S(1)}, s32[16]{0:T(128)}, u32[]{:S(2)}) copy-start(s32[16]{0:T(128)} %param.20) | copy-start | bytes 196
  3.1 6.7 %copy-start.11 = (s32[1,4]{1,0:T(1,128)S(1)}, s32[1,4]{1,0:T(1,128)}, u32[]{:S(2)}) copy-start(s32[1,4]{1,0:T(1,128)} %param.22) | copy-start | bytes 52
  4.0 13.8 %collective-permute-start = (bf16[2,1088,128]{2,1,0:T(8,128)(2,1)}, bf16[2,1088,128]{2,1,0:T(8,128)(2,1)}, u32[]{:S(2)}, u32[]{:S(2)}) collective-permute-start(bf16[2,1088,128]{2,1,0:T(8,128)(2,1)} %pad_maximum_fusion.5), channel_id=1, source_target_pairs={{0,2},{2,0},{4,6},{6,4},{8,10},{10,8},{12,14},{14,12},{1,3},{3,1},... | collective-permute-start | bytes 1671176 | tf_op jit(solution)/shard_map/ppermute | solution.py:435
  6.1 21.5 %collective-permute-start.10 = (bf16[2,1088,128]{2,1,0:T(8,128)(2,1)}, bf16[2,1088,128]{2,1,0:T(8,128)(2,1)}, u32[]{:S(2)}, u32[]{:S(2)}) collective-permute-start(bf16[2,1088,128]{2,1,0:T(8,128)(2,1)} %pad_maximum_fusion.6.refs_4_), channel_id=1, source_target_pairs={{4,8},{6,10},{8,4},{10,6},{5,9},{7,11},{9,5},{11,7},{20,24},{22,26... | collective-permute-start | bytes 1671176 | tf_op jit(solution)/shard_map/ppermute | solution.py:445
  9.3 26.5 %collective-permute-start.7 = (bf16[2,1088,128]{2,1,0:T(8,128)(2,1)}, bf16[2,1088,128]{2,1,0:T(8,128)(2,1)}, u32[]{:S(2)}, u32[]{:S(2)}) collective-permute-start(bf16[2,1088,128]{2,1,0:T(8,128)(2,1)} %pad_maximum_fusion.6.refs_4_), channel_id=1, source_target_pairs={{0,4},{2,6},{4,0},{6,2},{8,12},{10,14},{12,8},{14,10},{1,5},{3,7},... | collective-permute-start | bytes 1671176 | tf_op jit(solution)/shard_map/ppermute | solution.py:445
  11.8 3.0 %copy-start.12 = (s32[1,4]{1,0:T(1,128)S(1)}, s32[1,4]{1,0:T(1,128)}, u32[]{:S(2)}) copy-start(s32[1,4]{1,0:T(1,128)} %param.23) | copy-start | bytes 52
  13.3 32.0 %collective-permute-start.2 = (bf16[400,1024]{1,0:T(8,128)(2,1)}, bf16[400,1024]{1,0:T(8,128)(2,1)S(1)}, u32[]{:S(2)}, u32[]{:S(2)}) collective-permute-start(bf16[400,1024]{1,0:T(8,128)(2,1)} %get-tuple-element.72), channel_id=1, source_target_pairs={{0,16},{16,0},{1,17},{17,1},{2,18},{18,2},{3,19},{19,3},{4,20},{20... | collective-permute-start | bytes 2457608 | tf_op jit(solution)/shard_map/ppermute | solution.py:434
  17.8 15.2 %collective-permute-start.5 = (bf16[2,1088,128]{2,1,0:T(8,128)(2,1)}, bf16[2,1088,128]{2,1,0:T(8,128)(2,1)S(1)}, u32[]{:S(2)}, u32[]{:S(2)}) collective-permute-start(bf16[2,1088,128]{2,1,0:T(8,128)(2,1)} %collective-permute-done.refs_5_), channel_id=1, source_target_pairs={{4,8},{6,10},{8,4},{10,6},{5,9},{7,11},{9,5},{11,7},{20,24},{22,26... | collective-permute-start | bytes 1671176 | tf_op jit(solution)/shard_map/ppermute | solution.py:445
  21.0 16.6 %collective-permute-start.4 = (bf16[2,1088,128]{2,1,0:T(8,128)(2,1)}, bf16[2,1088,128]{2,1,0:T(8,128)(2,1)S(1)}, u32[]{:S(2)}, u32[]{:S(2)}) collective-permute-start(bf16[2,1088,128]{2,1,0:T(8,128)(2,1)} %collective-permute-done.refs_5_), channel_id=1, source_target_pairs={{0,4},{2,6},{4,0},{6,2},{8,12},{10,14},{12,8},{14,10},{1,5},{3,7},... | collective-permute-start | bytes 1671176 | tf_op jit(solution)/shard_map/ppermute | solution.py:445
  27.7 14.4 %collective-permute-start.6 = (bf16[2,2,64,128]{3,2,1,0:T(8,128)(2,1)S(1)}, bf16[2,2,64,128]{3,2,1,0:T(8,128)(2,1)S(1)}, u32[]{:S(2)}, u32[]{:S(2)}) collective-permute-start(bf16[2,2,64,128]{3,2,1,0:T(8,128)(2,1)S(1)} %pad_maximum_fusion.9), channel_id=1, source_target_pairs={{0,12},{2,14},{12,0},{14,2},{1,13},{3,15},{13,1},{15,3},{16,28},{1... | collective-permute-start | bytes 196616 | tf_op jit(solution)/shard_map/ppermute | solution.py:445
  33.0 9.0 %copy-start.7 = (bf16[2,1088,128]{2,1,0:T(8,128)(2,1)}, bf16[2,1088,128]{2,1,0:T(8,128)(2,1)S(1)}, u32[]{:S(2)}) copy-start(bf16[2,1088,128]{2,1,0:T(8,128)(2,1)S(1)} %collective-permute-done.5.refs_9_) | copy-start | bytes 1671172
  33.0 35.0 %collective-permute-start.1 = (bf16[400,1024]{1,0:T(8,128)(2,1)}, bf16[400,1024]{1,0:T(8,128)(2,1)}, u32[]{:S(2)}, u32[]{:S(2)}) collective-permute-start(bf16[400,1024]{1,0:T(8,128)(2,1)} %get-tuple-element.34), channel_id=1, source_target_pairs={{0,2},{2,0},{4,6},{6,4},{8,10},{10,8},{12,14},{14,12},{1,3},{3,1},... | collective-permute-start | bytes 2457608 | tf_op jit(solution)/shard_map/ppermute | solution.py:435
  35.9 32.1 %collective-permute-start.3 = (bf16[400,1024]{1,0:T(8,128)(2,1)}, bf16[400,1024]{1,0:T(8,128)(2,1)}, u32[]{:S(2)}, u32[]{:S(2)}) collective-permute-start(bf16[400,1024]{1,0:T(8,128)(2,1)} %get-tuple-element.35), channel_id=1, source_target_pairs={{0,18},{2,16},{4,22},{6,20},{8,26},{10,24},{12,30},{14,28},{16,2},... | collective-permute-start | bytes 2457608 | tf_op jit(solution)/shard_map/ppermute | solution.py:436
  37.6 4.5 %copy-start.8 = (bf16[2,1088,128]{2,1,0:T(8,128)(2,1)}, bf16[2,1088,128]{2,1,0:T(8,128)(2,1)S(1)}, u32[]{:S(2)}) copy-start(bf16[2,1088,128]{2,1,0:T(8,128)(2,1)S(1)} %collective-permute-done.4.refs_7_) | copy-start | bytes 1671172
  37.6 34.6 %collective-permute-start.11 = (bf16[2,2,1088,128]{3,2,1,0:T(8,128)(2,1)}, bf16[2,2,1088,128]{3,2,1,0:T(8,128)(2,1)}, u32[]{:S(2)}, u32[]{:S(2)}) collective-permute-start(bf16[2,2,1088,128]{3,2,1,0:T(8,128)(2,1)} %pad_maximum_fusion.4), channel_id=1, source_target_pairs={{4,0},{6,2},{8,12},{10,14},{5,1},{7,3},{9,13},{11,15},{20,16},{22,... | collective-permute-start | bytes 3342344 | tf_op jit(solution)/shard_map/ppermute | solution.py:445
  42.0 18.8 %copy-start.9 = (bf16[2,2,64,128]{3,2,1,0:T(8,128)(2,1)}, bf16[2,2,64,128]{3,2,1,0:T(8,128)(2,1)S(1)}, u32[]{:S(2)}) copy-start(bf16[2,2,64,128]{3,2,1,0:T(8,128)(2,1)S(1)} %collective-permute-done.6.refs_12_) | copy-start | bytes 196612
  42.1 26.6 %collective-permute-start.8 = (bf16[2,2,1088,128]{3,2,1,0:T(8,128)(2,1)}, bf16[2,2,1088,128]{3,2,1,0:T(8,128)(2,1)}, u32[]{:S(2)}, u32[]{:S(2)}) collective-permute-start(bf16[2,2,1088,128]{3,2,1,0:T(8,128)(2,1)} %pad_maximum_fusion.3), channel_id=1, source_target_pairs={{4,8},{6,10},{8,4},{10,6},{5,9},{7,11},{9,5},{11,7},{20,24},{22,26... | collective-permute-start | bytes 3342344 | tf_op jit(solution)/shard_map/ppermute | solution.py:445
  45.3 25.7 %copy-start.6 = (bf16[400,1024]{1,0:T(8,128)(2,1)}, bf16[400,1024]{1,0:T(8,128)(2,1)S(1)}, u32[]{:S(2)}) copy-start(bf16[400,1024]{1,0:T(8,128)(2,1)S(1)} %collective-permute-done.2.refs_2_) | copy-start | bytes 2457604
  68.7 28.4 %collective-permute-start.9 = (bf16[2,2,1088,128]{3,2,1,0:T(8,128)(2,1)}, bf16[2,2,1088,128]{3,2,1,0:T(8,128)(2,1)}, u32[]{:S(2)}, u32[]{:S(2)}) collective-permute-start(bf16[2,2,1088,128]{3,2,1,0:T(8,128)(2,1)} %collective-permute-done.8.refs_10_), channel_id=1, source_target_pairs={{4,0},{6,2},{8,12},{10,14},{5,1},{7,3},{9,13},{11,15},{20,16},{22,... | collective-permute-start | bytes 3342344 | tf_op jit(solution)/shard_map/ppermute | solution.py:445
  78.9 18.2 %collective-permute-start.12 = (bf16[4,64,128]{2,1,0:T(8,128)(2,1)}, bf16[4,64,128]{2,1,0:T(8,128)(2,1)S(1)}, u32[]{:S(2)}, u32[]{:S(2)}) collective-permute-start(bf16[4,64,128]{2,1,0:T(8,128)(2,1)} %get-tuple-element.53), channel_id=1, source_target_pairs={{0,2},{2,0},{4,6},{6,4},{8,10},{10,8},{12,14},{14,12},{1,3},{3,1},... | collective-permute-start | bytes 196616 | tf_op jit(solution)/shard_map/ppermute | solution.py:435
  80.2 16.9 %collective-permute-start.13 = (bf16[4,64,128]{2,1,0:T(8,128)(2,1)}, bf16[4,64,128]{2,1,0:T(8,128)(2,1)S(1)}, u32[]{:S(2)}, u32[]{:S(2)}) collective-permute-start(bf16[4,64,128]{2,1,0:T(8,128)(2,1)} %get-tuple-element.54), channel_id=1, source_target_pairs={{0,16},{16,0},{1,17},{17,1},{2,18},{18,2},{3,19},{19,3},{4,20},{20... | collective-permute-start | bytes 196616 | tf_op jit(solution)/shard_map/ppermute | solution.py:434
  81.4 15.7 %collective-permute-start.14 = (bf16[4,64,128]{2,1,0:T(8,128)(2,1)}, bf16[4,64,128]{2,1,0:T(8,128)(2,1)S(1)}, u32[]{:S(2)}, u32[]{:S(2)}) collective-permute-start(bf16[4,64,128]{2,1,0:T(8,128)(2,1)} %get-tuple-element.55), channel_id=1, source_target_pairs={{0,18},{2,16},{4,22},{6,20},{8,26},{10,24},{12,30},{14,28},{16,2},... | collective-permute-start | bytes 196616 | tf_op jit(solution)/shard_map/ppermute | solution.py:436
  101.5 17.9 %copy-start.2 = (bf16[384,2048]{1,0:T(8,128)(2,1)S(1)}, bf16[384,2048]{1,0:T(8,128)(2,1)}, u32[]{:S(2)}) copy-start(bf16[384,2048]{1,0:T(8,128)(2,1)} %q_ref.3) | copy-start | bytes 4718596
  101.5 17.9 %copy-start.3 = (f32[2,2,384,128]{3,2,1,0:T(8,128)S(1)}, f32[2,2,384,128]{3,2,1,0:T(8,128)}, u32[]{:S(2)}) copy-start(f32[2,2,384,128]{3,2,1,0:T(8,128)} %get-tuple-element.64.stat_ref) | copy-start | bytes 2359300
  101.5 17.9 %copy-start.4 = (bf16[4,64,128]{2,1,0:T(8,128)(2,1)S(1)}, bf16[4,64,128]{2,1,0:T(8,128)(2,1)}, u32[]{:S(2)}) copy-start(bf16[4,64,128]{2,1,0:T(8,128)(2,1)} %get-tuple-element.52.up0) | copy-start | bytes 196612
  101.5 17.9 %copy-start.5 = (s32[4,4]{1,0:T(4,128)S(1)}, s32[4,4]{1,0:T(4,128)}, u32[]{:S(2)}) copy-start(s32[4,4]{1,0:T(4,128)} %pad_add_fusion.info) | copy-start | bytes 196
  101.5 4.8 %collective-permute-start.15 = (f32[384,128]{1,0:T(8,128)}, f32[384,128]{1,0:T(8,128)S(1)}, u32[]{:S(2)}, u32[]{:S(2)}) collective-permute-start(f32[384,128]{1,0:T(8,128)} %get-tuple-element.61), channel_id=1, source_target_pairs={{0,2},{2,0},{4,6},{6,4},{8,10},{10,8},{12,14},{14,12},{1,3},{3,1},... | collective-permute-start | bytes 589832 | tf_op jit(solution)/shard_map/ppermute | solution.py:435
  102.4 6.5 %collective-permute-start.16 = (f32[384,128]{1,0:T(8,128)}, f32[384,128]{1,0:T(8,128)S(1)}, u32[]{:S(2)}, u32[]{:S(2)}) collective-permute-start(f32[384,128]{1,0:T(8,128)} %get-tuple-element.62), channel_id=1, source_target_pairs={{0,16},{16,0},{1,17},{17,1},{2,18},{18,2},{3,19},{19,3},{4,20},{20... | collective-permute-start | bytes 589832 | tf_op jit(solution)/shard_map/ppermute | solution.py:434
  105.6 5.8 %collective-permute-start.17 = (f32[384,128]{1,0:T(8,128)}, f32[384,128]{1,0:T(8,128)S(1)}, u32[]{:S(2)}, u32[]{:S(2)}) collective-permute-start(f32[384,128]{1,0:T(8,128)} %get-tuple-element.63), channel_id=1, source_target_pairs={{0,18},{2,16},{4,22},{6,20},{8,26},{10,24},{12,30},{14,28},{16,2},... | collective-permute-start | bytes 589832 | tf_op jit(solution)/shard_map/ppermute | solution.py:436
  112.4 7.1 %collective-permute-start.18 = (f32[384,128]{1,0:T(8,128)S(1)}, f32[384,128]{1,0:T(8,128)S(1)}, u32[]{:S(2)}, u32[]{:S(2)}) collective-permute-start(f32[384,128]{1,0:T(8,128)S(1)} %add_add_fusion.mine_ref), channel_id=1, source_target_pairs={{0,1},{1,0},{2,3},{3,2},{4,5},{5,4},{6,7},{7,6},{8,9},{9,8},{10,11... | collective-permute-start | bytes 589832 | tf_op jit(solution)/shard_map/ppermute | solution.py:526
  119.4 1.9 %copy-start.1 = (f32[2,384,1024]{2,1,0:T(8,128)S(1)}, f32[2,384,1024]{2,1,0:T(8,128)}, u32[]{:S(2)}) copy-start(f32[2,384,1024]{2,1,0:T(8,128)} %get-tuple-element.51.acc_ref) | copy-start | bytes 9437188
  (1 other events, 1.6 us)
where the time goes:
time: 133 us; the launch traced here: 130 us
  Pallas kernels  50.9 us (38%)
  starting transfers between devices  32.6 us (25%)
  waiting for transfers between devices  13.7 us (10%)
  other arithmetic  13.1 us (10%)
  matrix products  11.6 us (9%)
  local copies, waits for them, and re-layouts  7.16 us (5%)
    pallas_call x2, Pallas kernels, cached_attention(): pl.pallas_call(cached_kernel, grid_spec=pltpu.PrefetchScalarGridSpec(num_...  31 us
    ppermute x8, starting transfers between devices, body(): lax.ppermute(a, 'replica', [(2 * f + p, 2 * t + p) for f, t in pairs for...  15 us
    pallas_call x2, Pallas kernels, low_rank_step(): pl.pallas_call(functools.partial(low_rank_kernel, pick, len(pieces)), in_...  11.1 us
    pallas_call x1, Pallas kernels, final_step(): pl.pallas_call(final_kernel, grid_spec=pltpu.PrefetchScalarGridSpec(num_s...  8.81 us
    ppermute x1, starting transfers between devices, body(): low_other = lax.ppermute(low_sum, 'tensor', [(0, 1), (1, 0)])  6 us
    dot_general x1, matrix products, body(): jnp.dot(tokens_later, key_weight_matrix, preferred_element_type=jnp.float32)  5.8 us
    dot_general x1, matrix products, body(): jnp.dot(after(tokens, cached[0]), value_weight_matrix, preferred_element_...  5.79 us
    ppermute x3, starting transfers between devices, body(): by_x = lambda a: lax.ppermute(a, 'groups', [(0, 1), (1, 0)])  5.65 us
  transfers between devices with their start and end apart: 19, of which 7 were waited for; matrix products, arithmetic and copies ran while one was open for 20% of the time, Pallas kernels for 29%

commit v1 on v0

--- a/solution.py
+++ b/solution.py
@@ -33,9 +33,16 @@
     return lax.dot_general(a, b, (((1,), (1,)), ((), ())), preferred_element_type=jnp.float32)
 
 
-def cached_kernel(info, q_ref, k_ref, v_ref, *rest):
+def cached_kernel(first, carry_on, info, q_ref, k_ref, v_ref, *rest):
     acc_ref, stat_ref = rest[-2:]
-    r = pl.program_id(0)
+    r = pl.program_id(0) + first
+    if carry_on:
+
+        @pl.when(pl.program_id(0) == 0)
+        def _():
+            acc_ref[...] = rest[0][...]
+            stat_ref[...] = rest[1][...]
+
     rows_all = q_ref.shape[0]
     start = info[0, r]
     count = info[1, r]
@@ -94,23 +101,25 @@
             lax.fori_loop(0, tiles, functools.partial(tile, n * CHUNK), 0)
 
 
-def cached_attention(info, queries, cache_key, cache_value, part, before):
+def cached_attention(info, queries, cache_key, cache_value, part, before, first=0, many=REQ):
     rows = queries.shape[0]
     wide = PART * HEAD
     parts = queries.shape[1] // wide
     head = part * PART // GROUP
     slots = cache_key.shape[1]
     extra = [] if before is None else list(before)
+    carry_on = first > 0
     acc_spec = pl.BlockSpec((1, rows, wide), lambda r, s: (part, 0, 0))
     stat_spec = pl.BlockSpec((1, 2, rows, 128), lambda r, s: (part, 0, 0, 0))
-    cache = pl.BlockSpec((1, slots, HEAD), lambda r, s: (r, 0, head))
+    cache = pl.BlockSpec((1, slots, HEAD), lambda r, s: (r + first, 0, head))
+    aliased = [acc_spec, stat_spec] if carry_on else [pl.BlockSpec(memory_space=pltpu.HBM)] * 2
     return pl.pallas_call(
-        cached_kernel,
+        functools.partial(cached_kernel, first, carry_on),
         grid_spec=pltpu.PrefetchScalarGridSpec(
             num_scalar_prefetch=1,
-            grid=(REQ,),
+            grid=(many,),
             in_specs=[pl.BlockSpec((rows, wide), lambda r, s: (0, part)), cache, cache]
-            + [pl.BlockSpec(memory_space=pltpu.HBM)] * len(extra),
+            + (aliased if extra else []),
             out_specs=[acc_spec, stat_spec],
         ),
         out_shape=[
@@ -137,13 +146,7 @@
     rows, width = token_scr.shape[1:]
     held = piece_scr.shape[1]
     column = pl.multiple_of(place[2] * width, 128)
-    copies = [
-        pltpu.make_async_copy(tokens[0].at[:, pl.ds(column, width)], token_scr.at[0], sems.at[0])
-    ]
-    for n in range(1, 4):
-        copies.append(
-            pltpu.make_async_copy(tokens[n].at[pl.ds(0, rows)], token_scr.at[n], sems.at[n])
-        )
+    copies = []
     at = 0
     for p in range(n_pieces):
         if len(pieces[p].shape) == 4:
@@ -152,11 +155,20 @@
         else:
             target = piece_scr.at[at]
             at += 1
-        copies.append(pltpu.make_async_copy(pieces[p], target, sems.at[4 + p]))
-    for copy in copies:
+        copies.append(pltpu.make_async_copy(pieces[p], target, sems.at[8 + p]))
+    sources = [tokens[0].at[:, pl.ds(column, width)]]
+    sources += [tokens[n].at[pl.ds(0, rows)] for n in range(1, 4)]
+    of_chip = [
+        [pltpu.make_async_copy(sources[n], token_scr.at[n], sems.at[n])] for n in range(4)
+    ]
+    if pick == "late":
+        for n in range(4):
+            of_chip[n].append(pltpu.make_async_copy(before[n], outs[n], sems.at[4 + n]))
+    for copy in copies + [c for n in range(4) for c in of_chip[n]]:
         copy.start()
-    for n in range(4):
-        outs[n][...] = jnp.zeros_like(outs[n]) if pick == "early" else before[n][...]
+    if pick == "early":
+        for n in range(4):
+            outs[n][...] = jnp.zeros_like(outs[n])
     for copy in copies:
         copy.wait()
     window = rows // 3 + ALIGN
@@ -166,10 +178,26 @@
 
     for n in range(4):
 
-        def one(r, start):
+        def product(start, count, index, place_in):
+            base = pl.multiple_of(jnp.minimum((start // ALIGN) * ALIGN, rows - window), ALIGN)
+            span = pl.ds(base, window)
+            low = jnp.dot(
+                token_scr[n, span, :],
+                piece_scr[index, place_in, :width, :],
+                preferred_element_type=jnp.float32,
+            )
+            mine = (row_iota + base >= start) & (row_iota + base < start + count)
+            outs[n][span, :] = jnp.where(mine, low, outs[n][span, :])
+
+        for copy in of_chip[n]:
+            copy.wait()
+        found = [[jnp.int32(0)] * 3 for _ in range(2)]
+        start = jnp.int32(0)
+        for r in range(REQ):
             count = infos[n, r]
             slot = infos[n, REQ + r]
             owner = slot // held
+            place_in = slot % held
             layer = owner // 2
             other = jnp.where(owner % 2 != y, 1, 0)
             mates = layer // 2 == z // 2
@@ -179,41 +207,19 @@
                 kind = jnp.where(at_end, 4, jnp.where(ends, 3, 2))
                 kind = jnp.where(mates, jnp.where(layer == z, 0, 1), kind)
                 index = kind * 2 + other
-                valid = jnp.logical_not(last)
-            else:
-                index = other
-                valid = last
-
-            def product():
-                base = pl.multiple_of(
-                    jnp.minimum((start // ALIGN) * ALIGN, rows - window), ALIGN
-                )
-                span = pl.ds(base, window)
-                low = jnp.dot(
-                    token_scr[n, span, :],
-                    piece_scr[index, slot % held, :width, :],
-                    preferred_element_type=jnp.float32,
-                )
-                mine = (row_iota + base >= start) & (row_iota + base < start + count) & valid
-                outs[n][span, :] = jnp.where(mine, low, outs[n][span, :])
-
-            if pick == "early":
-                product()
+                product(start, jnp.where(last, 0, count), index, place_in)
                 outs[4 + n][r] = jnp.where(
-                    last,
-                    before[0][other, slot % held],
-                    piece_scr[index, slot % held, width:, :],
+                    last, before[0][other, place_in], piece_scr[index, place_in, width:, :]
                 )
             else:
-                pl.when(valid)(product)
-            return start + count
-
-        if pick == "early":
-            start = jnp.int32(0)
-            for r in range(REQ):
-                start = one(r, start)
-        else:
-            lax.fori_loop(0, REQ, one, 0)
+                for o in range(2):
+                    here = last & (other == o)
+                    fresh = (start, count, place_in)
+                    found[o] = [jnp.where(here, f, g) for f, g in zip(fresh, found[o])]
+            start = start + count
+        if pick == "late":
+            for o in range(2):
+                product(found[o][0], found[o][1], o, found[o][2])
 
 
 def low_rank_step(pick, place, infos, tokens, pieces, before, width):
@@ -228,13 +234,15 @@
         ups = [jax.ShapeDtypeStruct((REQ, tall - width, rank), jnp.bfloat16)] * 4
     return pl.pallas_call(
         functools.partial(low_rank_kernel, pick, len(pieces)),
-        in_specs=[smem, smem] + [hbm] * (4 + len(pieces)) + [vmem] * len(before),
+        in_specs=[smem, smem]
+        + [hbm] * (4 + len(pieces))
+        + [vmem if pick == "early" else hbm] * len(before),
         out_specs=[vmem] * (4 + len(ups)),
         out_shape=[jax.ShapeDtypeStruct((rows, rank), jnp.float32)] * 4 + ups,
         scratch_shapes=[
             pltpu.VMEM((4, rows, width), jnp.bfloat16),
             pltpu.VMEM((total, held, tall, rank), jnp.bfloat16),
-            pltpu.SemaphoreType.DMA((4 + len(pieces),)),
+            pltpu.SemaphoreType.DMA((8 + len(pieces),)),
         ],
         compiler_params=params(),
         cost_estimate=pl.CostEstimate(
@@ -478,8 +486,8 @@
         pair_b = in_pair(own_b)
         mid_b = across(own_b)
         plain_key = jnp.dot(tokens_later, key_weight_matrix, preferred_element_type=jnp.float32)
-        part = lambda n, q, b: cached_attention(
-            info, q, stored_key_cache, stored_value_cache, n, b
+        part = lambda n, q, b, *span: cached_attention(
+            info, q, stored_key_cache, stored_value_cache, n, b, *span
         )
         across_2 = across(after(jnp.stack([pair_a, pair_b]), plain_key))
         outward_2 = outward(after(jnp.stack([mid_a, mid_b]), plain_key))
@@ -497,10 +505,13 @@
         early = [own_a, own_b, pair_a, pair_b, mid_a, mid_b, across_2, outward_2]
         low = low_rank_step("early", place, infos, layer_tokens, early, [far_up], quarter)
         ups = [low[4], by_y(low[5]), by_x(low[6]), by_xy(low[7])]
-        cached = part(1, after(queries, low[0]), cached)
+        cached = part(1, after(queries, low[0]), cached, 0, REQ // 2)
         outward_3 = after(outward_3, cached[0], *ups)
         low = low_rank_step("late", place, infos, layer_tokens, [outward_3], low[:4], quarter)
-        low_sum = low[0] + by_y(low[1]) + by_x(low[2]) + by_xy(low[3])
+        cached = part(1, after(queries, low[0]), cached, REQ // 2, REQ // 2)
+        got = [by_y(low[1]), by_x(low[2]), by_xy(low[3])]
+        got = [after(g, cached[0]) for g in got]
+        low_sum = low[0] + got[0] + got[1] + got[2]
     else:
         down_all = lax.all_gather(adapter_down_weight, "replica", axis=0, tiled=True)
         mine = lax.dynamic_slice_in_dim(tokens, core * half, half, 1)

time: 133 us -> 131 us (0.985)
  the two profiles are of different devices: /device:TPU:9 before, /device:TPU:0 now
where the time goes in v1:
time: 131 us
  Pallas kernels  60.9 us (46%)
  starting transfers between devices  32.6 us (25%)
  other arithmetic  12.3 us (9%)
  matrix products  11.6 us (9%)
  local copies, waits for them, and re-layouts  7.16 us (5%)
  waiting for transfers between devices  4.99 us (4%)
    pallas_call x3, Pallas kernels, cached_attention(): pl.pallas_call(functools.partial(cached_kernel, first, carry_on), grid_sp...  41 us
    ppermute x8, starting transfers between devices, body(): lax.ppermute(a, 'replica', [(2 * f + p, 2 * t + p) for f, t in pairs for...  17.9 us
    pallas_call x2, Pallas kernels, low_rank_step(): pl.pallas_call(functools.partial(low_rank_kernel, pick, len(pieces)), in_...  11 us
    pallas_call x1, Pallas kernels, final_step(): pl.pallas_call(final_kernel, grid_spec=pltpu.PrefetchScalarGridSpec(num_s...  8.83 us
    ppermute x4, starting transfers between devices, body(): lax.ppermute(a, 'replica', [(r, r ^ 1) for r in range(n_replica)])  7.71 us
    dot_general x1, matrix products, body(): jnp.dot(after(tokens, cached[0]), value_weight_matrix, preferred_element_...  5.79 us
    dot_general x1, matrix products, body(): jnp.dot(tokens_later, key_weight_matrix, preferred_element_type=jnp.float32)  5.79 us
    ppermute x3, starting transfers between devices, body(): by_x = lambda a: lax.ppermute(a, 'groups', [(0, 1), (1, 0)])  4.49 us
  transfers between devices with their start and end apart: 19, of which 3 were waited for; matrix products, arithmetic and copies ran while one was open for 20% of the time, Pallas kernels for 36%

profile of v1, /device:TPU:0, one launch (start us, length us, event | category | flops | bytes accessed | tf_op | source)
XLA Modules:
  0.0 130.6 jit_solution(5998198016928309624)
XLA Ops:
  0.7 1.5 %copy-done = bf16[2,4096,128]{2,1,0:T(8,128)(2,1)S(1)} copy-done((bf16[2,4096,128]{2,1,0:T(8,128)(2,1)S(1)}, bf16[2,4096,128]{2,1,0:T(8,128)(2,1)}, u32[]{:S(2)}) %copy-start) | copy-done | bytes 2097176
  4.0 3.0 %collective-permute-start = (bf16[2,1088,128]{2,1,0:T(8,128)(2,1)}, bf16[2,1088,128]{2,1,0:T(8,128)(2,1)}, u32[]{:S(2)}, u32[]{:S(2)}) collective-permute-start(bf16[2,1088,128]{2,1,0:T(8,128)(2,1)} %pad_maximum_fusion.5), channel_id=1, source_target_pairs={{0,2},{2,0},{4,6},{6,4},{8,10},{10,8},{12,14},{14,12},{1,3},{3,1},... | collective-permute-start | bytes 1671176 | tf_op jit(solution)/shard_map/ppermute | solution.py:443
  7.0 0.9 pad_maximum_fusion.6.refs_4_
  7.8 1.5 %collective-permute-start.10 = (bf16[2,1088,128]{2,1,0:T(8,128)(2,1)}, bf16[2,1088,128]{2,1,0:T(8,128)(2,1)}, u32[]{:S(2)}, u32[]{:S(2)}) collective-permute-start(bf16[2,1088,128]{2,1,0:T(8,128)(2,1)} %pad_maximum_fusion.6.refs_4_), channel_id=1, source_target_pairs={{4,8},{6,10},{8,4},{10,6},{5,9},{7,11},{9,5},{11,7},{20,24},{22,26... | collective-permute-start | bytes 1671176 | tf_op jit(solution)/shard_map/ppermute | solution.py:453
  9.3 3.6 %collective-permute-start.7 = (bf16[2,1088,128]{2,1,0:T(8,128)(2,1)}, bf16[2,1088,128]{2,1,0:T(8,128)(2,1)}, u32[]{:S(2)}, u32[]{:S(2)}) collective-permute-start(bf16[2,1088,128]{2,1,0:T(8,128)(2,1)} %pad_maximum_fusion.6.refs_4_), channel_id=1, source_target_pairs={{0,4},{2,6},{4,0},{6,2},{8,12},{10,14},{12,8},{14,10},{1,5},{3,7},... | collective-permute-start | bytes 1671176 | tf_op jit(solution)/shard_map/ppermute | solution.py:453
  13.5 1.8 %constant_dynamic-slice_fusion.1 = (bf16[384,1024]{1,0:T(8,128)(2,1)S(1)}, bf16[384,1024]{1,0:T(8,128)(2,1)S(1)}, bf16[384,1024]{1,0:T(8,128)(2,1)S(1)}) fusion(bf16[384,8192]{1,0:T(8,128)(2,1)} %refs_0_.3, s32[]{:T(128)S(6)} %select_n.82, s32[]{:T(128)S(6)} %select_n.81, s32[]{:T(128)S(6)} %select_n.80), kind=kLoop, calls=%fused_computation.38 | loop fusion | bytes 4718604 | tf_op jit(solution)/shard_map/dynamic_slice | solution.py:477
  15.3 1.5 %pad_maximum_fusion = (bf16[400,1024]{1,0:T(8,128)(2,1)}, bf16[400,1024]{1,0:T(8,128)(2,1)}, bf16[400,1024]{1,0:T(8,128)(2,1)}) fusion(bf16[16,1024]{1,0:T(8,128)(2,1)S(1)} %fusion.6, bf16[384,1024]{1,0:T(8,128)(2,1)S(1)} %get-tuple-element.77, bf16[384,1024]{1,0:T(8,128)(2,1)S(1)} %get-tuple-element.78, bf16[384,1024]{1,0:T(8,128)(2,1)S(1)} %get-tuple-element.79), kind=kLoop, calls=%fused_computation | loop fusion | flops 4096000 | bytes 4849664 | tf_op jit(solution)/shard_map/concatenate | solution.py:476
  16.8 1.5 %collective-permute-start.2 = (bf16[400,1024]{1,0:T(8,128)(2,1)}, bf16[400,1024]{1,0:T(8,128)(2,1)S(1)}, u32[]{:S(2)}, u32[]{:S(2)}) collective-permute-start(bf16[400,1024]{1,0:T(8,128)(2,1)} %get-tuple-element.84), channel_id=1, source_target_pairs={{0,16},{16,0},{1,17},{17,1},{2,18},{18,2},{3,19},{19,3},{4,20},{20... | collective-permute-start | bytes 2457608 | tf_op jit(solution)/shard_map/ppermute | solution.py:442
  20.6 4.6 %collective-permute-start.4 = (bf16[2,1088,128]{2,1,0:T(8,128)(2,1)}, bf16[2,1088,128]{2,1,0:T(8,128)(2,1)S(1)}, u32[]{:S(2)}, u32[]{:S(2)}) collective-permute-start(bf16[2,1088,128]{2,1,0:T(8,128)(2,1)} %collective-permute-done.refs_5_), channel_id=1, source_target_pairs={{0,4},{2,6},{4,0},{6,2},{8,12},{10,14},{12,8},{14,10},{1,5},{3,7},... | collective-permute-start | bytes 1671176 | tf_op jit(solution)/shard_map/ppermute | solution.py:453
  25.2 5.8 %fusion.9.pk_ref = f32[384,256]{1,0:T(8,128)S(1)} fusion(bf16[384,8192]{1,0:T(8,128)(2,1)} %refs_0_.3, bf16[8192,256]{1,0:T(8,128)(2,1)} %param.16), kind=kOutput, calls=%fused_computation.54 | convolution fusion | flops 1610612736 | bytes 10878976 | tf_op jit(solution)/shard_map/dot_general | solution.py:488
  31.8 3.3 %collective-permute-start.6 = (bf16[2,2,64,128]{3,2,1,0:T(8,128)(2,1)S(1)}, bf16[2,2,64,128]{3,2,1,0:T(8,128)(2,1)S(1)}, u32[]{:S(2)}, u32[]{:S(2)}) collective-permute-start(bf16[2,2,64,128]{3,2,1,0:T(8,128)(2,1)S(1)} %pad_maximum_fusion.9), channel_id=1, source_target_pairs={{0,12},{2,14},{12,0},{14,2},{1,13},{3,15},{13,1},{15,3},{16,28},{1... | collective-permute-start | bytes 196616 | tf_op jit(solution)/shard_map/ppermute | solution.py:453
  35.1 1.6 %collective-permute-start.1 = (bf16[400,1024]{1,0:T(8,128)(2,1)}, bf16[400,1024]{1,0:T(8,128)(2,1)}, u32[]{:S(2)}, u32[]{:S(2)}) collective-permute-start(bf16[400,1024]{1,0:T(8,128)(2,1)} %get-tuple-element.40), channel_id=1, source_target_pairs={{0,2},{2,0},{4,6},{6,4},{8,10},{10,8},{12,14},{14,12},{1,3},{3,1},... | collective-permute-start | bytes 2457608 | tf_op jit(solution)/shard_map/ppermute | solution.py:443
  36.7 2.2 %pad_maximum_fusion.4 = bf16[2,2,1088,128]{3,2,1,0:T(8,128)(2,1)} fusion(bf16[1,2,1088,128]{3,2,1,0:T(8,128)(2,1)S(1)} %bitcast.28, bf16[1,2,1088,128]{3,2,1,0:T(8,128)(2,1)} %bitcast.13), kind=kLoop, calls=%fused_computation.4 | loop fusion | flops 557056 | bytes 2228224 | tf_op jit(solution)/shard_map/stack | solution.py:493
  38.8 1.4 %collective-permute-start.3 = (bf16[400,1024]{1,0:T(8,128)(2,1)}, bf16[400,1024]{1,0:T(8,128)(2,1)}, u32[]{:S(2)}, u32[]{:S(2)}) collective-permute-start(bf16[400,1024]{1,0:T(8,128)(2,1)} %get-tuple-element.41), channel_id=1, source_target_pairs={{0,18},{2,16},{4,22},{6,20},{8,26},{10,24},{12,30},{14,28},{16,2},... | collective-permute-start | bytes 2457608 | tf_op jit(solution)/shard_map/ppermute | solution.py:444
  40.3 1.3 collective-permute-start.11
  41.6 2.1 %pad_maximum_fusion.3 = bf16[2,2,1088,128]{3,2,1,0:T(8,128)(2,1)} fusion(bf16[1,2,1088,128]{3,2,1,0:T(8,128)(2,1)S(1)} %bitcast.29, bf16[1,2,1088,128]{3,2,1,0:T(8,128)(2,1)} %bitcast.11), kind=kLoop, calls=%fused_computation.3 | loop fusion | flops 557056 | bytes 2228224 | tf_op jit(solution)/shard_map/stack | solution.py:492
  43.7 1.7 %collective-permute-start.8 = (bf16[2,2,1088,128]{3,2,1,0:T(8,128)(2,1)}, bf16[2,2,1088,128]{3,2,1,0:T(8,128)(2,1)}, u32[]{:S(2)}, u32[]{:S(2)}) collective-permute-start(bf16[2,2,1088,128]{3,2,1,0:T(8,128)(2,1)} %pad_maximum_fusion.3), channel_id=1, source_target_pairs={{4,8},{6,10},{8,4},{10,6},{5,9},{7,11},{9,5},{11,7},{20,24},{22,26... | collective-permute-start | bytes 3342344 | tf_op jit(solution)/shard_map/ppermute | solution.py:453
  45.5 18.3 %cached_attention.3 = (f32[2,384,1024]{2,1,0:T(8,128)}, f32[2,2,384,128]{3,2,1,0:T(8,128)}) custom-call(s32[4,4]{1,0:T(4,128)} %pad_add_fusion.info, bf16[384,2048]{1,0:T(8,128)(2,1)} %q_ref.4, bf16[4,2048,256]{2,1,0:T(8,128)(2,1)} %k_ref.5, bf16[4,2048,256]{2,1,0:T(8,128)(2,1)} %v_ref.5), custom_call_target="tpu_custom_call" | custom-call | flops 6442450944 | bytes 6291456 | tf_op jit(solution)/shard_map/cached_attention/pallas_call | solution.py:116
  63.8 5.8 %fusion.10.pv_ref = f32[384,256]{1,0:T(8,128)S(1)} fusion(bf16[384,8192]{1,0:T(8,128)(2,1)} %refs_0_.3, bf16[8192,256]{1,0:T(8,128)(2,1)} %param.17), kind=kOutput, calls=%fused_computation.55 | convolution fusion | flops 1610612736 | bytes 10878976 | tf_op jit(solution)/shard_map/dot_general | solution.py:496
  69.6 1.7 %collective-permute-done.1.refs_1_ = bf16[400,1024]{1,0:T(8,128)(2,1)} collective-permute-done((bf16[400,1024]{1,0:T(8,128)(2,1)}, bf16[400,1024]{1,0:T(8,128)(2,1)}, u32[]{:S(2)}, u32[]{:S(2)}) %collective-permute-start.1) | collective-permute-done | bytes 819232 | tf_op jit(solution)/shard_map/ppermute | solution.py:443
  72.0 1.3 collective-permute-start.9
  74.6 6.5 %low_rank_early.1 = (f32[384,128]{1,0:T(8,128)}, f32[384,128]{1,0:T(8,128)}, f32[384,128]{1,0:T(8,128)}, f32[384,128]{1,0:T(8,128)}, bf16[4,64,128]{2,1,0:T(8,12...) custom-call(s32[3]{0:T(128)} %pad_add_fusion.2.place, ...), custom_call_target="tpu_custom_call" | custom-call | flops 1610612736 | bytes 6291456 | tf_op jit(solution)/shard_map/low_rank_early/pallas_call | solution.py:235
  81.1 1.6 %collective-permute-start.12 = (bf16[4,64,128]{2,1,0:T(8,128)(2,1)}, bf16[4,64,128]{2,1,0:T(8,128)(2,1)S(1)}, u32[]{:S(2)}, u32[]{:S(2)}) collective-permute-start(bf16[4,64,128]{2,1,0:T(8,128)(2,1)} %get-tuple-element.59), channel_id=1, source_target_pairs={{0,2},{2,0},{4,6},{6,4},{8,10},{10,8},{12,14},{14,12},{1,3},{3,1},... | collective-permute-start | bytes 196616 | tf_op jit(solution)/shard_map/ppermute | solution.py:443
  82.7 1.5 %collective-permute-start.13 = (bf16[4,64,128]{2,1,0:T(8,128)(2,1)}, bf16[4,64,128]{2,1,0:T(8,128)(2,1)S(1)}, u32[]{:S(2)}, u32[]{:S(2)}) collective-permute-start(bf16[4,64,128]{2,1,0:T(8,128)(2,1)} %get-tuple-element.60), channel_id=1, source_target_pairs={{0,16},{16,0},{1,17},{17,1},{2,18},{18,2},{3,19},{19,3},{4,20},{20... | collective-permute-start | bytes 196616 | tf_op jit(solution)/shard_map/ppermute | solution.py:442
  84.7 10.4 %cached_attention.4 = (f32[2,384,1024]{2,1,0:T(8,128)}, f32[2,2,384,128]{3,2,1,0:T(8,128)}) custom-call(s32[4,4]{1,0:T(4,128)} %pad_add_fusion.info, bf16[384,2048]{1,0:T(8,128)(2,1)} %q_ref.4, bf16[4,2048,256]{2,1,0:T(8,128)(2,1)} %k_ref.5, bf16[4,2048,256]{2,1,0:T(8,128)(2,1)} %v_ref.5, ...), custom_call_target="tpu_custom_call", output_to_operand_aliasing={{0}: (4, {}), {1}: (5, {})} | custom-call | flops 6442450944 | bytes 6291456 | tf_op jit(solution)/shard_map/cached_attention/pallas_call | solution.py:116
  95.1 2.8 %collective-permute-done.9.refs_4_ = bf16[2,2,1088,128]{3,2,1,0:T(8,128)(2,1)} collective-permute-done((bf16[2,2,1088,128]{3,2,1,0:T(8,128)(2,1)}, bf16[2,2,1088,128]{3,2,1,0:T(8,128)(2,1)}, u32[]{:S(2)}, u32[]{:S(2)}) %collective-permute-start.9) | collective-permute-done | bytes 1114144 | tf_op jit(solution)/shard_map/ppermute | solution.py:453
  97.9 4.5 %low_rank_late.1 = (f32[384,128]{1,0:T(8,128)}, f32[384,128]{1,0:T(8,128)}, f32[384,128]{1,0:T(8,128)}, f32[384,128]{1,0:T(8,128)}) custom-call(s32[3]{0:T(128)} %pad_add_fusion.2.place, s32[4,8]{1,0:T(4,128)} %pad_add_fusion.1.infos, bf16[384,8192]{1,0:T(8,128)(2,1)} %refs_0_.3, bf16[400,1024]{1,0:T(8,128)(2,1)} %collective-permute-done.1.refs_1_, ...), custom_call_target="tpu_custom_call" | custom-call | flops 1610612736 | bytes 6291456 | tf_op jit(solution)/shard_map/low_rank_late/pallas_call | solution.py:235
  102.4 1.6 %collective-permute-start.15 = (f32[384,128]{1,0:T(8,128)}, f32[384,128]{1,0:T(8,128)S(1)}, u32[]{:S(2)}, u32[]{:S(2)}) collective-permute-start(f32[384,128]{1,0:T(8,128)} %get-tuple-element.67), channel_id=1, source_target_pairs={{0,2},{2,0},{4,6},{6,4},{8,10},{10,8},{12,14},{14,12},{1,3},{3,1},... | collective-permute-start | bytes 589832 | tf_op jit(solution)/shard_map/ppermute | solution.py:443
  104.0 1.5 %collective-permute-start.16 = (f32[384,128]{1,0:T(8,128)}, f32[384,128]{1,0:T(8,128)S(1)}, u32[]{:S(2)}, u32[]{:S(2)}) collective-permute-start(f32[384,128]{1,0:T(8,128)} %get-tuple-element.72), channel_id=1, source_target_pairs={{0,16},{16,0},{1,17},{17,1},{2,18},{18,2},{3,19},{19,3},{4,20},{20... | collective-permute-start | bytes 589832 | tf_op jit(solution)/shard_map/ppermute | solution.py:442
  106.0 12.2 %cached_attention.5 = (f32[2,384,1024]{2,1,0:T(8,128)}, f32[2,2,384,128]{3,2,1,0:T(8,128)}) custom-call(s32[4,4]{1,0:T(4,128)} %pad_add_fusion.info, bf16[384,2048]{1,0:T(8,128)(2,1)} %q_ref.4, bf16[4,2048,256]{2,1,0:T(8,128)(2,1)} %k_ref.5, bf16[4,2048,256]{2,1,0:T(8,128)(2,1)} %v_ref.5, ...), custom_call_target="tpu_custom_call", output_to_operand_aliasing={{0}: (4, {}), {1}: (5, {})} | custom-call | flops 6442450944 | bytes 6291456 | tf_op jit(solution)/shard_map/cached_attention/pallas_call | solution.py:116
  119.8 1.9 %copy-done.1 = f32[2,384,1024]{2,1,0:T(8,128)S(1)} copy-done((f32[2,384,1024]{2,1,0:T(8,128)S(1)}, f32[2,384,1024]{2,1,0:T(8,128)}, u32[]{:S(2)}) %copy-start.1) | copy-done | bytes 3145752
  121.7 8.8 %final_step.1 = (bf16[384,2048]{1,0:T(8,128)(2,1)}, bf16[384,256]{1,0:T(8,128)(2,1)}, bf16[384,256]{1,0:T(8,128)(2,1)}) custom-call(s32[4,4]{1,0:T(4,128)S(1)} %copy-done.5, f32[384,128]{1,0:T(8,128)S(1)} %add_add_fusion.mine_ref, f32[384,128]{1,0:T(8,128)S(1)} %collective-permute-done.18.other_ref, f32[384,256]{1,0:T(8,128)S(1)} %fusion.9.pk_ref, ...), custom_call_target="tpu_custom_call" | custom-call | tf_op jit(solution)/shard_map/final_step/pallas_call | solution.py:351
  (80 shorter events, 9.8 us)
Async XLA Ops:
  3.1 9.9 %copy-start.11 = (s32[8,4]{0,1:T(4,128)S(1)}, s32[8,4]{0,1:T(4,128)}, u32[]{:S(2)}) copy-start(s32[8,4]{0,1:T(4,128)} %param.21) | copy-start | bytes 388
  3.1 10.0 %copy-start.14 = (s32[16]{0:T(128)S(1)}, s32[16]{0:T(128)}, u32[]{:S(2)}) copy-start(s32[16]{0:T(128)} %param.20) | copy-start | bytes 196
  3.1 10.2 %copy-start.12 = (s32[1,4]{1,0:T(1,128)S(1)}, s32[1,4]{1,0:T(1,128)}, u32[]{:S(2)}) copy-start(s32[1,4]{1,0:T(1,128)} %param.22) | copy-start | bytes 52
  4.0 15.9 %collective-permute-start = (bf16[2,1088,128]{2,1,0:T(8,128)(2,1)}, bf16[2,1088,128]{2,1,0:T(8,128)(2,1)}, u32[]{:S(2)}, u32[]{:S(2)}) collective-permute-start(bf16[2,1088,128]{2,1,0:T(8,128)(2,1)} %pad_maximum_fusion.5), channel_id=1, source_target_pairs={{0,2},{2,0},{4,6},{6,4},{8,10},{10,8},{12,14},{14,12},{1,3},{3,1},... | collective-permute-start | bytes 1671176 | tf_op jit(solution)/shard_map/ppermute | solution.py:443
  7.8 24.0 %collective-permute-start.10 = (bf16[2,1088,128]{2,1,0:T(8,128)(2,1)}, bf16[2,1088,128]{2,1,0:T(8,128)(2,1)}, u32[]{:S(2)}, u32[]{:S(2)}) collective-permute-start(bf16[2,1088,128]{2,1,0:T(8,128)(2,1)} %pad_maximum_fusion.6.refs_4_), channel_id=1, source_target_pairs={{4,8},{6,10},{8,4},{10,6},{5,9},{7,11},{9,5},{11,7},{20,24},{22,26... | collective-permute-start | bytes 1671176 | tf_op jit(solution)/shard_map/ppermute | solution.py:453
  9.3 29.5 %collective-permute-start.7 = (bf16[2,1088,128]{2,1,0:T(8,128)(2,1)}, bf16[2,1088,128]{2,1,0:T(8,128)(2,1)}, u32[]{:S(2)}, u32[]{:S(2)}) collective-permute-start(bf16[2,1088,128]{2,1,0:T(8,128)(2,1)} %pad_maximum_fusion.6.refs_4_), channel_id=1, source_target_pairs={{0,4},{2,6},{4,0},{6,2},{8,12},{10,14},{12,8},{14,10},{1,5},{3,7},... | collective-permute-start | bytes 1671176 | tf_op jit(solution)/shard_map/ppermute | solution.py:453
  15.3 3.4 %copy-start.13 = (s32[1,4]{1,0:T(1,128)S(1)}, s32[1,4]{1,0:T(1,128)}, u32[]{:S(2)}) copy-start(s32[1,4]{1,0:T(1,128)} %param.23) | copy-start | bytes 52
  16.8 28.7 %collective-permute-start.2 = (bf16[400,1024]{1,0:T(8,128)(2,1)}, bf16[400,1024]{1,0:T(8,128)(2,1)S(1)}, u32[]{:S(2)}, u32[]{:S(2)}) collective-permute-start(bf16[400,1024]{1,0:T(8,128)(2,1)} %get-tuple-element.84), channel_id=1, source_target_pairs={{0,16},{16,0},{1,17},{17,1},{2,18},{18,2},{3,19},{19,3},{4,20},{20... | collective-permute-start | bytes 2457608 | tf_op jit(solution)/shard_map/ppermute | solution.py:442
  19.9 15.2 %collective-permute-start.5 = (bf16[2,1088,128]{2,1,0:T(8,128)(2,1)}, bf16[2,1088,128]{2,1,0:T(8,128)(2,1)S(1)}, u32[]{:S(2)}, u32[]{:S(2)}) collective-permute-start(bf16[2,1088,128]{2,1,0:T(8,128)(2,1)} %collective-permute-done.refs_5_), channel_id=1, source_target_pairs={{4,8},{6,10},{8,4},{10,6},{5,9},{7,11},{9,5},{11,7},{20,24},{22,26... | collective-permute-start | bytes 1671176 | tf_op jit(solution)/shard_map/ppermute | solution.py:453
  20.6 19.7 %collective-permute-start.4 = (bf16[2,1088,128]{2,1,0:T(8,128)(2,1)}, bf16[2,1088,128]{2,1,0:T(8,128)(2,1)S(1)}, u32[]{:S(2)}, u32[]{:S(2)}) collective-permute-start(bf16[2,1088,128]{2,1,0:T(8,128)(2,1)} %collective-permute-done.refs_5_), channel_id=1, source_target_pairs={{0,4},{2,6},{4,0},{6,2},{8,12},{10,14},{12,8},{14,10},{1,5},{3,7},... | collective-permute-start | bytes 1671176 | tf_op jit(solution)/shard_map/ppermute | solution.py:453
  31.8 11.9 %collective-permute-start.6 = (bf16[2,2,64,128]{3,2,1,0:T(8,128)(2,1)S(1)}, bf16[2,2,64,128]{3,2,1,0:T(8,128)(2,1)S(1)}, u32[]{:S(2)}, u32[]{:S(2)}) collective-permute-start(bf16[2,2,64,128]{3,2,1,0:T(8,128)(2,1)S(1)} %pad_maximum_fusion.9), channel_id=1, source_target_pairs={{0,12},{2,14},{12,0},{14,2},{1,13},{3,15},{13,1},{15,3},{16,28},{1... | collective-permute-start | bytes 196616 | tf_op jit(solution)/shard_map/ppermute | solution.py:453
  35.1 8.6 %copy-start.7 = (bf16[2,1088,128]{2,1,0:T(8,128)(2,1)}, bf16[2,1088,128]{2,1,0:T(8,128)(2,1)S(1)}, u32[]{:S(2)}) copy-start(bf16[2,1088,128]{2,1,0:T(8,128)(2,1)S(1)} %collective-permute-done.5.refs_9_) | copy-start | bytes 1671172
  35.1 36.2 %collective-permute-start.1 = (bf16[400,1024]{1,0:T(8,128)(2,1)}, bf16[400,1024]{1,0:T(8,128)(2,1)}, u32[]{:S(2)}, u32[]{:S(2)}) collective-permute-start(bf16[400,1024]{1,0:T(8,128)(2,1)} %get-tuple-element.40), channel_id=1, source_target_pairs={{0,2},{2,0},{4,6},{6,4},{8,10},{10,8},{12,14},{14,12},{1,3},{3,1},... | collective-permute-start | bytes 2457608 | tf_op jit(solution)/shard_map/ppermute | solution.py:443
  38.8 32.5 %collective-permute-start.3 = (bf16[400,1024]{1,0:T(8,128)(2,1)}, bf16[400,1024]{1,0:T(8,128)(2,1)}, u32[]{:S(2)}, u32[]{:S(2)}) collective-permute-start(bf16[400,1024]{1,0:T(8,128)(2,1)} %get-tuple-element.41), channel_id=1, source_target_pairs={{0,18},{2,16},{4,22},{6,20},{8,26},{10,24},{12,30},{14,28},{16,2},... | collective-permute-start | bytes 2457608 | tf_op jit(solution)/shard_map/ppermute | solution.py:444
  40.3 3.4 %copy-start.8 = (bf16[2,1088,128]{2,1,0:T(8,128)(2,1)}, bf16[2,1088,128]{2,1,0:T(8,128)(2,1)S(1)}, u32[]{:S(2)}) copy-start(bf16[2,1088,128]{2,1,0:T(8,128)(2,1)S(1)} %collective-permute-done.4.refs_7_) | copy-start | bytes 1671172
  40.3 34.3 %collective-permute-start.11 = (bf16[2,2,1088,128]{3,2,1,0:T(8,128)(2,1)}, bf16[2,2,1088,128]{3,2,1,0:T(8,128)(2,1)}, u32[]{:S(2)}, u32[]{:S(2)}) collective-permute-start(bf16[2,2,1088,128]{3,2,1,0:T(8,128)(2,1)} %pad_maximum_fusion.4), channel_id=1, source_target_pairs={{4,0},{6,2},{8,12},{10,14},{5,1},{7,3},{9,13},{11,15},{20,16},{22,... | collective-permute-start | bytes 3342344 | tf_op jit(solution)/shard_map/ppermute | solution.py:453
  43.7 20.1 %copy-start.10 = (bf16[2,2,64,128]{3,2,1,0:T(8,128)(2,1)}, bf16[2,2,64,128]{3,2,1,0:T(8,128)(2,1)S(1)}, u32[]{:S(2)}) copy-start(bf16[2,2,64,128]{3,2,1,0:T(8,128)(2,1)S(1)} %collective-permute-done.6.refs_12_) | copy-start | bytes 196612
  43.7 28.3 %collective-permute-start.8 = (bf16[2,2,1088,128]{3,2,1,0:T(8,128)(2,1)}, bf16[2,2,1088,128]{3,2,1,0:T(8,128)(2,1)}, u32[]{:S(2)}, u32[]{:S(2)}) collective-permute-start(bf16[2,2,1088,128]{3,2,1,0:T(8,128)(2,1)} %pad_maximum_fusion.3), channel_id=1, source_target_pairs={{4,8},{6,10},{8,4},{10,6},{5,9},{7,11},{9,5},{11,7},{20,24},{22,26... | collective-permute-start | bytes 3342344 | tf_op jit(solution)/shard_map/ppermute | solution.py:453
  45.5 27.8 %copy-start.6 = (bf16[400,1024]{1,0:T(8,128)(2,1)}, bf16[400,1024]{1,0:T(8,128)(2,1)S(1)}, u32[]{:S(2)}) copy-start(bf16[400,1024]{1,0:T(8,128)(2,1)S(1)} %collective-permute-done.2.refs_2_) | copy-start | bytes 2457604
  72.0 25.9 %collective-permute-start.9 = (bf16[2,2,1088,128]{3,2,1,0:T(8,128)(2,1)}, bf16[2,2,1088,128]{3,2,1,0:T(8,128)(2,1)}, u32[]{:S(2)}, u32[]{:S(2)}) collective-permute-start(bf16[2,2,1088,128]{3,2,1,0:T(8,128)(2,1)} %collective-permute-done.8.refs_10_), channel_id=1, source_target_pairs={{4,0},{6,2},{8,12},{10,14},{5,1},{7,3},{9,13},{11,15},{20,16},{22,... | collective-permute-start | bytes 3342344 | tf_op jit(solution)/shard_map/ppermute | solution.py:453
  81.1 14.0 %collective-permute-start.12 = (bf16[4,64,128]{2,1,0:T(8,128)(2,1)}, bf16[4,64,128]{2,1,0:T(8,128)(2,1)S(1)}, u32[]{:S(2)}, u32[]{:S(2)}) collective-permute-start(bf16[4,64,128]{2,1,0:T(8,128)(2,1)} %get-tuple-element.59), channel_id=1, source_target_pairs={{0,2},{2,0},{4,6},{6,4},{8,10},{10,8},{12,14},{14,12},{1,3},{3,1},... | collective-permute-start | bytes 196616 | tf_op jit(solution)/shard_map/ppermute | solution.py:443
  82.7 12.4 %collective-permute-start.13 = (bf16[4,64,128]{2,1,0:T(8,128)(2,1)}, bf16[4,64,128]{2,1,0:T(8,128)(2,1)S(1)}, u32[]{:S(2)}, u32[]{:S(2)}) collective-permute-start(bf16[4,64,128]{2,1,0:T(8,128)(2,1)} %get-tuple-element.60), channel_id=1, source_target_pairs={{0,16},{16,0},{1,17},{17,1},{2,18},{18,2},{3,19},{19,3},{4,20},{20... | collective-permute-start | bytes 196616 | tf_op jit(solution)/shard_map/ppermute | solution.py:442
  84.2 10.9 %collective-permute-start.14 = (bf16[4,64,128]{2,1,0:T(8,128)(2,1)}, bf16[4,64,128]{2,1,0:T(8,128)(2,1)S(1)}, u32[]{:S(2)}, u32[]{:S(2)}) collective-permute-start(bf16[4,64,128]{2,1,0:T(8,128)(2,1)} %get-tuple-element.61), channel_id=1, source_target_pairs={{0,18},{2,16},{4,22},{6,20},{8,26},{10,24},{12,30},{14,28},{16,2},... | collective-permute-start | bytes 196616 | tf_op jit(solution)/shard_map/ppermute | solution.py:444
  102.4 15.8 %collective-permute-start.15 = (f32[384,128]{1,0:T(8,128)}, f32[384,128]{1,0:T(8,128)S(1)}, u32[]{:S(2)}, u32[]{:S(2)}) collective-permute-start(f32[384,128]{1,0:T(8,128)} %get-tuple-element.67), channel_id=1, source_target_pairs={{0,2},{2,0},{4,6},{6,4},{8,10},{10,8},{12,14},{14,12},{1,3},{3,1},... | collective-permute-start | bytes 589832 | tf_op jit(solution)/shard_map/ppermute | solution.py:443
  104.0 14.3 %collective-permute-start.16 = (f32[384,128]{1,0:T(8,128)}, f32[384,128]{1,0:T(8,128)S(1)}, u32[]{:S(2)}, u32[]{:S(2)}) collective-permute-start(f32[384,128]{1,0:T(8,128)} %get-tuple-element.72), channel_id=1, source_target_pairs={{0,16},{16,0},{1,17},{17,1},{2,18},{18,2},{3,19},{19,3},{4,20},{20... | collective-permute-start | bytes 589832 | tf_op jit(solution)/shard_map/ppermute | solution.py:442
  105.5 12.8 %collective-permute-start.17 = (f32[384,128]{1,0:T(8,128)}, f32[384,128]{1,0:T(8,128)S(1)}, u32[]{:S(2)}, u32[]{:S(2)}) collective-permute-start(f32[384,128]{1,0:T(8,128)} %get-tuple-element.74), channel_id=1, source_target_pairs={{0,18},{2,16},{4,22},{6,20},{8,26},{10,24},{12,30},{14,28},{16,2},... | collective-permute-start | bytes 589832 | tf_op jit(solution)/shard_map/ppermute | solution.py:444
  106.0 12.3 %copy-start.9 = (f32[384,128]{1,0:T(8,128)S(1)}, f32[384,128]{1,0:T(8,128)}, u32[]{:S(2)}) copy-start(f32[384,128]{1,0:T(8,128)} %get-tuple-element.66) | copy-start | bytes 589828
  118.2 1.6 %copy-start.3 = (f32[2,2,384,128]{3,2,1,0:T(8,128)S(1)}, f32[2,2,384,128]{3,2,1,0:T(8,128)}, u32[]{:S(2)}) copy-start(f32[2,2,384,128]{3,2,1,0:T(8,128)} %get-tuple-element.76.stat_ref) | copy-start | bytes 2359300
  118.2 1.6 %copy-start.4 = (bf16[4,64,128]{2,1,0:T(8,128)(2,1)S(1)}, bf16[4,64,128]{2,1,0:T(8,128)(2,1)}, u32[]{:S(2)}) copy-start(bf16[4,64,128]{2,1,0:T(8,128)(2,1)} %get-tuple-element.58.up0) | copy-start | bytes 196612
  118.2 1.6 %copy-start.5 = (s32[4,4]{1,0:T(4,128)S(1)}, s32[4,4]{1,0:T(4,128)}, u32[]{:S(2)}) copy-start(s32[4,4]{1,0:T(4,128)} %pad_add_fusion.info) | copy-start | bytes 196
  118.3 1.5 %collective-permute-start.18 = (f32[384,128]{1,0:T(8,128)S(1)}, f32[384,128]{1,0:T(8,128)S(1)}, u32[]{:S(2)}, u32[]{:S(2)}) collective-permute-start(f32[384,128]{1,0:T(8,128)S(1)} %add_add_fusion.mine_ref), channel_id=1, source_target_pairs={{0,1},{1,0},{2,3},{3,2},{4,5},{5,4},{6,7},{7,6},{8,9},{9,8},{10,11... | collective-permute-start | bytes 589832 | tf_op jit(solution)/shard_map/ppermute | solution.py:537
  119.8 1.9 %copy-start.1 = (f32[2,384,1024]{2,1,0:T(8,128)S(1)}, f32[2,384,1024]{2,1,0:T(8,128)}, u32[]{:S(2)}) copy-start(f32[2,384,1024]{2,1,0:T(8,128)} %get-tuple-element.70.acc_ref) | copy-start | bytes 9437188
  (2 other events, 3.2 us)

commit v2 on v1

--- a/solution.py
+++ b/solution.py
@@ -489,8 +489,9 @@
         part = lambda n, q, b, *span: cached_attention(
             info, q, stored_key_cache, stored_value_cache, n, b, *span
         )
-        across_2 = across(after(jnp.stack([pair_a, pair_b]), plain_key))
-        outward_2 = outward(after(jnp.stack([mid_a, mid_b]), plain_key))
+        to_cross = after(jnp.stack([pair_a, pair_b]), plain_key)
+        across_2 = across(to_cross)
+        outward_2 = outward(after(jnp.stack([after(mid_a, to_cross), mid_b]), plain_key))
         cached = part(0, after(queries, pair_b, mid_b, far_up, t_x, plain_key), None)
         outward_3 = outward(after(across_2, cached[0]))
         plain_value = jnp.dot(

time: 131 us -> 131 us (level)
  the two profiles are of different devices: /device:TPU:0 before, /device:TPU:17 now
where the time goes in v2:
time: 131 us; the launch traced here: 130 us
  Pallas kernels  61.3 us (47%)
  starting transfers between devices  31.5 us (24%)
  other arithmetic  12.3 us (9%)
  matrix products  11.6 us (9%)
  local copies, waits for them, and re-layouts  7.16 us (5%)
  waiting for transfers between devices  5.47 us (4%)
    pallas_call x3, Pallas kernels, cached_attention(): pl.pallas_call(functools.partial(cached_kernel, first, carry_on), grid_sp...  41.4 us
    ppermute x8, starting transfers between devices, body(): lax.ppermute(a, 'replica', [(2 * f + p, 2 * t + p) for f, t in pairs for...  15.3 us
    pallas_call x2, Pallas kernels, low_rank_step(): pl.pallas_call(functools.partial(low_rank_kernel, pick, len(pieces)), in_...  11 us
    pallas_call x1, Pallas kernels, final_step(): pl.pallas_call(final_kernel, grid_spec=pltpu.PrefetchScalarGridSpec(num_s...  8.83 us
    dot_general x1, matrix products, body(): jnp.dot(tokens_later, key_weight_matrix, preferred_element_type=jnp.float32)  5.8 us
    dot_general x1, matrix products, body(): jnp.dot(after(tokens, cached[0]), value_weight_matrix, preferred_element_...  5.79 us
    ppermute x1, starting transfers between devices, body(): low_other = lax.ppermute(low_sum, 'tensor', [(0, 1), (1, 0)])  5.58 us
    ppermute x3, starting transfers between devices, body(): lax.ppermute(a, ('groups', 'replica'), [(g * n_replica + r, (1 - g) * n_r...  4.15 us
  transfers between devices with their start and end apart: 19, of which 4 were waited for; matrix products, arithmetic and copies ran while one was open for 20% of the time, Pallas kernels for 37%

profile of v2, /device:TPU:17, one launch (start us, length us, event | category | flops | bytes accessed | tf_op | source)
XLA Modules:
  0.0 130.3 jit_solution(12737877898530177745)
XLA Ops:
  0.7 1.5 %copy-done = bf16[2,4096,128]{2,1,0:T(8,128)(2,1)S(1)} copy-done((bf16[2,4096,128]{2,1,0:T(8,128)(2,1)S(1)}, bf16[2,4096,128]{2,1,0:T(8,128)(2,1)}, u32[]{:S(2)}) %copy-start) | copy-done | bytes 2097176
  4.0 1.2 collective-permute-start
  5.3 0.9 pad_maximum_fusion.6.refs_4_
  6.1 1.3 collective-permute-start.7
  7.4 1.9 %collective-permute-start.10 = (bf16[2,1088,128]{2,1,0:T(8,128)(2,1)}, bf16[2,1088,128]{2,1,0:T(8,128)(2,1)}, u32[]{:S(2)}, u32[]{:S(2)}) collective-permute-start(bf16[2,1088,128]{2,1,0:T(8,128)(2,1)} %pad_maximum_fusion.6.refs_4_), channel_id=1, source_target_pairs={{4,8},{6,10},{8,4},{10,6},{5,9},{7,11},{9,5},{11,7},{20,24},{22,26... | collective-permute-start | bytes 1671176 | tf_op jit(solution)/shard_map/ppermute | solution.py:453
  9.9 1.8 %constant_dynamic-slice_fusion.1 = (bf16[384,1024]{1,0:T(8,128)(2,1)S(1)}, bf16[384,1024]{1,0:T(8,128)(2,1)S(1)}, bf16[384,1024]{1,0:T(8,128)(2,1)S(1)}) fusion(bf16[384,8192]{1,0:T(8,128)(2,1)} %refs_0_.3, s32[]{:T(128)S(6)} %select_n.82, s32[]{:T(128)S(6)} %select_n.81, s32[]{:T(128)S(6)} %select_n.80), kind=kLoop, calls=%fused_computation.38 | loop fusion | bytes 4718604 | tf_op jit(solution)/shard_map/dynamic_slice | solution.py:477
  11.7 1.5 %pad_maximum_fusion = (bf16[400,1024]{1,0:T(8,128)(2,1)}, bf16[400,1024]{1,0:T(8,128)(2,1)}, bf16[400,1024]{1,0:T(8,128)(2,1)}) fusion(bf16[16,1024]{1,0:T(8,128)(2,1)S(1)} %fusion.6, bf16[384,1024]{1,0:T(8,128)(2,1)S(1)} %get-tuple-element.79, bf16[384,1024]{1,0:T(8,128)(2,1)S(1)} %get-tuple-element.80, bf16[384,1024]{1,0:T(8,128)(2,1)S(1)} %get-tuple-element.81), kind=kLoop, calls=%fused_computation | loop fusion | flops 4096000 | bytes 4849664 | tf_op jit(solution)/shard_map/concatenate | solution.py:476
  13.2 1.2 collective-permute-start.2
  16.0 1.8 %collective-permute-done.refs_5_ = bf16[2,1088,128]{2,1,0:T(8,128)(2,1)} collective-permute-done((bf16[2,1088,128]{2,1,0:T(8,128)(2,1)}, bf16[2,1088,128]{2,1,0:T(8,128)(2,1)}, u32[]{:S(2)}, u32[]{:S(2)}) %collective-permute-start) | collective-permute-done | bytes 557088 | tf_op jit(solution)/shard_map/ppermute | solution.py:443
  17.8 1.3 collective-permute-start.4
  19.1 1.9 %collective-permute-start.5 = (bf16[2,1088,128]{2,1,0:T(8,128)(2,1)}, bf16[2,1088,128]{2,1,0:T(8,128)(2,1)S(1)}, u32[]{:S(2)}, u32[]{:S(2)}) collective-permute-start(bf16[2,1088,128]{2,1,0:T(8,128)(2,1)} %collective-permute-done.refs_5_), channel_id=1, source_target_pairs={{4,8},{6,10},{8,4},{10,6},{5,9},{7,11},{9,5},{11,7},{20,24},{22,26... | collective-permute-start | bytes 1671176 | tf_op jit(solution)/shard_map/ppermute | solution.py:453
  21.0 5.8 %fusion.9.pk_ref = f32[384,256]{1,0:T(8,128)S(1)} fusion(bf16[384,8192]{1,0:T(8,128)(2,1)} %refs_0_.3, bf16[8192,256]{1,0:T(8,128)(2,1)} %param.16), kind=kOutput, calls=%fused_computation.54 | convolution fusion | flops 1610612736 | bytes 10878976 | tf_op jit(solution)/shard_map/dot_general | solution.py:488
  28.3 2.8 %collective-permute-done.4.refs_7_ = bf16[2,1088,128]{2,1,0:T(8,128)(2,1)S(1)} collective-permute-done((bf16[2,1088,128]{2,1,0:T(8,128)(2,1)}, bf16[2,1088,128]{2,1,0:T(8,128)(2,1)S(1)}, u32[]{:S(2)}, u32[]{:S(2)}) %collective-permute-start.4) | collective-permute-done | bytes 557088 | tf_op jit(solution)/shard_map/ppermute | solution.py:453
  31.8 2.1 %pad_maximum_fusion.3 = bf16[2,2,1088,128]{3,2,1,0:T(8,128)(2,1)} fusion(bf16[1,2,1088,128]{3,2,1,0:T(8,128)(2,1)S(1)} %bitcast.28, bf16[1,2,1088,128]{3,2,1,0:T(8,128)(2,1)} %bitcast.11), kind=kLoop, calls=%fused_computation.3 | loop fusion | flops 557056 | bytes 2228224 | tf_op jit(solution)/shard_map/stack | solution.py:492
  34.0 1.7 %collective-permute-start.3 = (bf16[400,1024]{1,0:T(8,128)(2,1)}, bf16[400,1024]{1,0:T(8,128)(2,1)}, u32[]{:S(2)}, u32[]{:S(2)}) collective-permute-start(bf16[400,1024]{1,0:T(8,128)(2,1)} %get-tuple-element.42), channel_id=1, source_target_pairs={{0,18},{2,16},{4,22},{6,20},{8,26},{10,24},{12,30},{14,28},{16,2},... | collective-permute-start | bytes 2457608 | tf_op jit(solution)/shard_map/ppermute | solution.py:444
  35.6 2.1 %collective-permute-start.8 = (bf16[2,2,1088,128]{3,2,1,0:T(8,128)(2,1)}, bf16[2,2,1088,128]{3,2,1,0:T(8,128)(2,1)}, u32[]{:S(2)}, u32[]{:S(2)}) collective-permute-start(bf16[2,2,1088,128]{3,2,1,0:T(8,128)(2,1)} %pad_maximum_fusion.3), channel_id=1, source_target_pairs={{4,8},{6,10},{8,4},{10,6},{5,9},{7,11},{9,5},{11,7},{20,24},{22,26... | collective-permute-start | bytes 3342344 | tf_op jit(solution)/shard_map/ppermute | solution.py:453
  37.7 2.2 %pad_maximum_fusion.4 = bf16[2,2,1088,128]{3,2,1,0:T(8,128)(2,1)} fusion(bf16[1,2,1088,128]{3,2,1,0:T(8,128)(2,1)S(1)} %bitcast.29, bf16[1,2,1088,128]{3,2,1,0:T(8,128)(2,1)} %bitcast.13), kind=kLoop, calls=%fused_computation.4 | loop fusion | flops 557056 | bytes 2228224 | tf_op jit(solution)/shard_map/stack | solution.py:494
  39.9 3.8 %collective-permute-start.11 = (bf16[2,2,1088,128]{3,2,1,0:T(8,128)(2,1)}, bf16[2,2,1088,128]{3,2,1,0:T(8,128)(2,1)}, u32[]{:S(2)}, u32[]{:S(2)}) collective-permute-start(bf16[2,2,1088,128]{3,2,1,0:T(8,128)(2,1)} %pad_maximum_fusion.4), channel_id=1, source_target_pairs={{4,0},{6,2},{8,12},{10,14},{5,1},{7,3},{9,13},{11,15},{20,16},{22,... | collective-permute-start | bytes 3342344 | tf_op jit(solution)/shard_map/ppermute | solution.py:453
  43.7 18.5 %cached_attention.3 = (f32[2,384,1024]{2,1,0:T(8,128)}, f32[2,2,384,128]{3,2,1,0:T(8,128)}) custom-call(s32[4,4]{1,0:T(4,128)} %pad_add_fusion.info, bf16[384,2048]{1,0:T(8,128)(2,1)} %q_ref.4, bf16[4,2048,256]{2,1,0:T(8,128)(2,1)} %k_ref.5, bf16[4,2048,256]{2,1,0:T(8,128)(2,1)} %v_ref.5), custom_call_target="tpu_custom_call" | custom-call | flops 6442450944 | bytes 6291456 | tf_op jit(solution)/shard_map/cached_attention/pallas_call | solution.py:116
  62.3 5.8 %fusion.10.pv_ref = f32[384,256]{1,0:T(8,128)S(1)} fusion(bf16[384,8192]{1,0:T(8,128)(2,1)} %refs_0_.3, bf16[8192,256]{1,0:T(8,128)(2,1)} %param.17), kind=kOutput, calls=%fused_computation.55 | convolution fusion | flops 1610612736 | bytes 10878976 | tf_op jit(solution)/shard_map/dot_general | solution.py:497
  68.8 2.3 %collective-permute-start.9 = (bf16[2,2,1088,128]{3,2,1,0:T(8,128)(2,1)}, bf16[2,2,1088,128]{3,2,1,0:T(8,128)(2,1)}, u32[]{:S(2)}, u32[]{:S(2)}) collective-permute-start(bf16[2,2,1088,128]{3,2,1,0:T(8,128)(2,1)} %collective-permute-done.8.refs_10_), channel_id=1, source_target_pairs={{4,0},{6,2},{8,12},{10,14},{5,1},{7,3},{9,13},{11,15},{20,16},{22,... | collective-permute-start | bytes 3342344 | tf_op jit(solution)/shard_map/ppermute | solution.py:453
  72.4 6.5 %low_rank_early.1 = (f32[384,128]{1,0:T(8,128)}, f32[384,128]{1,0:T(8,128)}, f32[384,128]{1,0:T(8,128)}, f32[384,128]{1,0:T(8,128)}, bf16[4,64,128]{2,1,0:T(8,12...) custom-call(s32[3]{0:T(128)} %pad_add_fusion.2.place, ...), custom_call_target="tpu_custom_call" | custom-call | flops 1610612736 | bytes 6291456 | tf_op jit(solution)/shard_map/low_rank_early/pallas_call | solution.py:235
  79.1 1.2 collective-permute-start.13
  80.3 1.4 %collective-permute-start.14 = (bf16[4,64,128]{2,1,0:T(8,128)(2,1)}, bf16[4,64,128]{2,1,0:T(8,128)(2,1)S(1)}, u32[]{:S(2)}, u32[]{:S(2)}) collective-permute-start(bf16[4,64,128]{2,1,0:T(8,128)(2,1)} %get-tuple-element.63), channel_id=1, source_target_pairs={{0,18},{2,16},{4,22},{6,20},{8,26},{10,24},{12,30},{14,28},{16,2},... | collective-permute-start | bytes 196616 | tf_op jit(solution)/shard_map/ppermute | solution.py:444
  81.6 8.4 %cached_attention.4 = (f32[2,384,1024]{2,1,0:T(8,128)}, f32[2,2,384,128]{3,2,1,0:T(8,128)}) custom-call(s32[4,4]{1,0:T(4,128)} %pad_add_fusion.info, bf16[384,2048]{1,0:T(8,128)(2,1)} %q_ref.4, bf16[4,2048,256]{2,1,0:T(8,128)(2,1)} %k_ref.5, bf16[4,2048,256]{2,1,0:T(8,128)(2,1)} %v_ref.5, ...), custom_call_target="tpu_custom_call", output_to_operand_aliasing={{0}: (4, {}), {1}: (5, {})} | custom-call | flops 6442450944 | bytes 6291456 | tf_op jit(solution)/shard_map/cached_attention/pallas_call | solution.py:116
  90.7 4.5 %low_rank_late.1 = (f32[384,128]{1,0:T(8,128)}, f32[384,128]{1,0:T(8,128)}, f32[384,128]{1,0:T(8,128)}, f32[384,128]{1,0:T(8,128)}) custom-call(s32[3]{0:T(128)} %pad_add_fusion.2.place, s32[4,8]{1,0:T(4,128)} %pad_add_fusion.1.infos, bf16[384,8192]{1,0:T(8,128)(2,1)} %refs_0_.3, bf16[400,1024]{1,0:T(8,128)(2,1)} %collective-permute-done.1.refs_1_, ...), custom_call_target="tpu_custom_call" | custom-call | flops 1610612736 | bytes 6291456 | tf_op jit(solution)/shard_map/low_rank_late/pallas_call | solution.py:235
  95.9 1.3 collective-permute-start.16
  97.2 1.1 collective-permute-start.17
  98.3 14.5 %cached_attention.5 = (f32[2,384,1024]{2,1,0:T(8,128)}, f32[2,2,384,128]{3,2,1,0:T(8,128)}) custom-call(s32[4,4]{1,0:T(4,128)} %pad_add_fusion.info, bf16[384,2048]{1,0:T(8,128)(2,1)} %q_ref.4, bf16[4,2048,256]{2,1,0:T(8,128)(2,1)} %k_ref.5, bf16[4,2048,256]{2,1,0:T(8,128)(2,1)} %v_ref.5, ...), custom_call_target="tpu_custom_call", output_to_operand_aliasing={{0}: (4, {}), {1}: (5, {})} | custom-call | flops 6442450944 | bytes 6291456 | tf_op jit(solution)/shard_map/cached_attention/pallas_call | solution.py:116
  112.9 5.6 %collective-permute-start.18 = (f32[384,128]{1,0:T(8,128)S(1)}, f32[384,128]{1,0:T(8,128)S(1)}, u32[]{:S(2)}, u32[]{:S(2)}) collective-permute-start(f32[384,128]{1,0:T(8,128)S(1)} %add_add_fusion.mine_ref), channel_id=1, source_target_pairs={{0,1},{1,0},{2,3},{3,2},{4,5},{5,4},{6,7},{7,6},{8,9},{9,8},{10,11... | collective-permute-start | bytes 589832 | tf_op jit(solution)/shard_map/ppermute | solution.py:538
  119.6 1.9 %copy-done.1 = f32[2,384,1024]{2,1,0:T(8,128)S(1)} copy-done((f32[2,384,1024]{2,1,0:T(8,128)S(1)}, f32[2,384,1024]{2,1,0:T(8,128)}, u32[]{:S(2)}) %copy-start.1) | copy-done | bytes 3145752
  121.5 8.8 %final_step.1 = (bf16[384,2048]{1,0:T(8,128)(2,1)}, bf16[384,256]{1,0:T(8,128)(2,1)}, bf16[384,256]{1,0:T(8,128)(2,1)}) custom-call(s32[4,4]{1,0:T(4,128)S(1)} %copy-done.5, f32[384,128]{1,0:T(8,128)S(1)} %add_add_fusion.mine_ref, f32[384,128]{1,0:T(8,128)S(1)} %collective-permute-done.18.other_ref, f32[384,256]{1,0:T(8,128)S(1)} %fusion.9.pk_ref, ...), custom_call_target="tpu_custom_call" | custom-call | tf_op jit(solution)/shard_map/final_step/pallas_call | solution.py:351
  (80 shorter events, 10.6 us)
Async XLA Ops:
  3.1 6.3 %copy-start.11 = (s32[8,4]{0,1:T(4,128)S(1)}, s32[8,4]{0,1:T(4,128)}, u32[]{:S(2)}) copy-start(s32[8,4]{0,1:T(4,128)} %param.21) | copy-start | bytes 388
  3.1 6.4 %copy-start.14 = (s32[16]{0:T(128)S(1)}, s32[16]{0:T(128)}, u32[]{:S(2)}) copy-start(s32[16]{0:T(128)} %param.20) | copy-start | bytes 196
  3.1 6.6 %copy-start.12 = (s32[1,4]{1,0:T(1,128)S(1)}, s32[1,4]{1,0:T(1,128)}, u32[]{:S(2)}) copy-start(s32[1,4]{1,0:T(1,128)} %param.22) | copy-start | bytes 52
  4.0 13.8 %collective-permute-start = (bf16[2,1088,128]{2,1,0:T(8,128)(2,1)}, bf16[2,1088,128]{2,1,0:T(8,128)(2,1)}, u32[]{:S(2)}, u32[]{:S(2)}) collective-permute-start(bf16[2,1088,128]{2,1,0:T(8,128)(2,1)} %pad_maximum_fusion.5), channel_id=1, source_target_pairs={{0,2},{2,0},{4,6},{6,4},{8,10},{10,8},{12,14},{14,12},{1,3},{3,1},... | collective-permute-start | bytes 1671176 | tf_op jit(solution)/shard_map/ppermute | solution.py:443
  6.1 21.5 %collective-permute-start.7 = (bf16[2,1088,128]{2,1,0:T(8,128)(2,1)}, bf16[2,1088,128]{2,1,0:T(8,128)(2,1)}, u32[]{:S(2)}, u32[]{:S(2)}) collective-permute-start(bf16[2,1088,128]{2,1,0:T(8,128)(2,1)} %pad_maximum_fusion.6.refs_4_), channel_id=1, source_target_pairs={{0,4},{2,6},{4,0},{6,2},{8,12},{10,14},{12,8},{14,10},{1,5},{3,7},... | collective-permute-start | bytes 1671176 | tf_op jit(solution)/shard_map/ppermute | solution.py:453
  7.4 26.6 %collective-permute-start.10 = (bf16[2,1088,128]{2,1,0:T(8,128)(2,1)}, bf16[2,1088,128]{2,1,0:T(8,128)(2,1)}, u32[]{:S(2)}, u32[]{:S(2)}) collective-permute-start(bf16[2,1088,128]{2,1,0:T(8,128)(2,1)} %pad_maximum_fusion.6.refs_4_), channel_id=1, source_target_pairs={{4,8},{6,10},{8,4},{10,6},{5,9},{7,11},{9,5},{11,7},{20,24},{22,26... | collective-permute-start | bytes 1671176 | tf_op jit(solution)/shard_map/ppermute | solution.py:453
  11.7 3.1 %copy-start.13 = (s32[1,4]{1,0:T(1,128)S(1)}, s32[1,4]{1,0:T(1,128)}, u32[]{:S(2)}) copy-start(s32[1,4]{1,0:T(1,128)} %param.23) | copy-start | bytes 52
  13.2 30.5 %collective-permute-start.2 = (bf16[400,1024]{1,0:T(8,128)(2,1)}, bf16[400,1024]{1,0:T(8,128)(2,1)S(1)}, u32[]{:S(2)}, u32[]{:S(2)}) collective-permute-start(bf16[400,1024]{1,0:T(8,128)(2,1)} %get-tuple-element.86), channel_id=1, source_target_pairs={{0,16},{16,0},{1,17},{17,1},{2,18},{18,2},{3,19},{19,3},{4,20},{20... | collective-permute-start | bytes 2457608 | tf_op jit(solution)/shard_map/ppermute | solution.py:442
  17.8 13.3 %collective-permute-start.4 = (bf16[2,1088,128]{2,1,0:T(8,128)(2,1)}, bf16[2,1088,128]{2,1,0:T(8,128)(2,1)S(1)}, u32[]{:S(2)}, u32[]{:S(2)}) collective-permute-start(bf16[2,1088,128]{2,1,0:T(8,128)(2,1)} %collective-permute-done.refs_5_), channel_id=1, source_target_pairs={{0,4},{2,6},{4,0},{6,2},{8,12},{10,14},{12,8},{14,10},{1,5},{3,7},... | collective-permute-start | bytes 1671176 | tf_op jit(solution)/shard_map/ppermute | solution.py:453
  19.1 16.6 %collective-permute-start.5 = (bf16[2,1088,128]{2,1,0:T(8,128)(2,1)}, bf16[2,1088,128]{2,1,0:T(8,128)(2,1)S(1)}, u32[]{:S(2)}, u32[]{:S(2)}) collective-permute-start(bf16[2,1088,128]{2,1,0:T(8,128)(2,1)} %collective-permute-done.refs_5_), channel_id=1, source_target_pairs={{4,8},{6,10},{8,4},{10,6},{5,9},{7,11},{9,5},{11,7},{20,24},{22,26... | collective-permute-start | bytes 1671176 | tf_op jit(solution)/shard_map/ppermute | solution.py:453
  27.6 12.3 %collective-permute-start.6 = (bf16[2,2,64,128]{3,2,1,0:T(8,128)(2,1)S(1)}, bf16[2,2,64,128]{3,2,1,0:T(8,128)(2,1)S(1)}, u32[]{:S(2)}, u32[]{:S(2)}) collective-permute-start(bf16[2,2,64,128]{3,2,1,0:T(8,128)(2,1)S(1)} %pad_maximum_fusion.9), channel_id=1, source_target_pairs={{0,12},{2,14},{12,0},{14,2},{1,13},{3,15},{13,1},{15,3},{16,28},{1... | collective-permute-start | bytes 196616 | tf_op jit(solution)/shard_map/ppermute | solution.py:453
  31.1 8.8 %copy-start.7 = (bf16[2,1088,128]{2,1,0:T(8,128)(2,1)}, bf16[2,1088,128]{2,1,0:T(8,128)(2,1)S(1)}, u32[]{:S(2)}) copy-start(bf16[2,1088,128]{2,1,0:T(8,128)(2,1)S(1)} %collective-permute-done.4.refs_7_) | copy-start | bytes 1671172
  31.1 37.0 %collective-permute-start.1 = (bf16[400,1024]{1,0:T(8,128)(2,1)}, bf16[400,1024]{1,0:T(8,128)(2,1)}, u32[]{:S(2)}, u32[]{:S(2)}) collective-permute-start(bf16[400,1024]{1,0:T(8,128)(2,1)} %get-tuple-element.41), channel_id=1, source_target_pairs={{0,2},{2,0},{4,6},{6,4},{8,10},{10,8},{12,14},{14,12},{1,3},{3,1},... | collective-permute-start | bytes 2457608 | tf_op jit(solution)/shard_map/ppermute | solution.py:443
  34.0 34.1 %collective-permute-start.3 = (bf16[400,1024]{1,0:T(8,128)(2,1)}, bf16[400,1024]{1,0:T(8,128)(2,1)}, u32[]{:S(2)}, u32[]{:S(2)}) collective-permute-start(bf16[400,1024]{1,0:T(8,128)(2,1)} %get-tuple-element.42), channel_id=1, source_target_pairs={{0,18},{2,16},{4,22},{6,20},{8,26},{10,24},{12,30},{14,28},{16,2},... | collective-permute-start | bytes 2457608 | tf_op jit(solution)/shard_map/ppermute | solution.py:444
  35.6 4.2 %copy-start.8 = (bf16[2,1088,128]{2,1,0:T(8,128)(2,1)}, bf16[2,1088,128]{2,1,0:T(8,128)(2,1)S(1)}, u32[]{:S(2)}) copy-start(bf16[2,1088,128]{2,1,0:T(8,128)(2,1)S(1)} %collective-permute-done.5.refs_9_) | copy-start | bytes 1671172
  35.6 33.1 %collective-permute-start.8 = (bf16[2,2,1088,128]{3,2,1,0:T(8,128)(2,1)}, bf16[2,2,1088,128]{3,2,1,0:T(8,128)(2,1)}, u32[]{:S(2)}, u32[]{:S(2)}) collective-permute-start(bf16[2,2,1088,128]{3,2,1,0:T(8,128)(2,1)} %pad_maximum_fusion.3), channel_id=1, source_target_pairs={{4,8},{6,10},{8,4},{10,6},{5,9},{7,11},{9,5},{11,7},{20,24},{22,26... | collective-permute-start | bytes 3342344 | tf_op jit(solution)/shard_map/ppermute | solution.py:453
  39.9 22.4 %copy-start.10 = (bf16[2,2,64,128]{3,2,1,0:T(8,128)(2,1)}, bf16[2,2,64,128]{3,2,1,0:T(8,128)(2,1)S(1)}, u32[]{:S(2)}) copy-start(bf16[2,2,64,128]{3,2,1,0:T(8,128)(2,1)S(1)} %collective-permute-done.6.refs_12_) | copy-start | bytes 196612
  39.9 32.5 %collective-permute-start.11 = (bf16[2,2,1088,128]{3,2,1,0:T(8,128)(2,1)}, bf16[2,2,1088,128]{3,2,1,0:T(8,128)(2,1)}, u32[]{:S(2)}, u32[]{:S(2)}) collective-permute-start(bf16[2,2,1088,128]{3,2,1,0:T(8,128)(2,1)} %pad_maximum_fusion.4), channel_id=1, source_target_pairs={{4,0},{6,2},{8,12},{10,14},{5,1},{7,3},{9,13},{11,15},{20,16},{22,... | collective-permute-start | bytes 3342344 | tf_op jit(solution)/shard_map/ppermute | solution.py:453
  43.7 27.4 %copy-start.6 = (bf16[400,1024]{1,0:T(8,128)(2,1)}, bf16[400,1024]{1,0:T(8,128)(2,1)S(1)}, u32[]{:S(2)}) copy-start(bf16[400,1024]{1,0:T(8,128)(2,1)S(1)} %collective-permute-done.2.refs_2_) | copy-start | bytes 2457604
  68.8 22.0 %collective-permute-start.9 = (bf16[2,2,1088,128]{3,2,1,0:T(8,128)(2,1)}, bf16[2,2,1088,128]{3,2,1,0:T(8,128)(2,1)}, u32[]{:S(2)}, u32[]{:S(2)}) collective-permute-start(bf16[2,2,1088,128]{3,2,1,0:T(8,128)(2,1)} %collective-permute-done.8.refs_10_), channel_id=1, source_target_pairs={{4,0},{6,2},{8,12},{10,14},{5,1},{7,3},{9,13},{11,15},{20,16},{22,... | collective-permute-start | bytes 3342344 | tf_op jit(solution)/shard_map/ppermute | solution.py:453
  78.9 11.1 %collective-permute-start.12 = (bf16[4,64,128]{2,1,0:T(8,128)(2,1)}, bf16[4,64,128]{2,1,0:T(8,128)(2,1)S(1)}, u32[]{:S(2)}, u32[]{:S(2)}) collective-permute-start(bf16[4,64,128]{2,1,0:T(8,128)(2,1)} %get-tuple-element.61), channel_id=1, source_target_pairs={{0,2},{2,0},{4,6},{6,4},{8,10},{10,8},{12,14},{14,12},{1,3},{3,1},... | collective-permute-start | bytes 196616 | tf_op jit(solution)/shard_map/ppermute | solution.py:443
  79.1 11.0 %collective-permute-start.13 = (bf16[4,64,128]{2,1,0:T(8,128)(2,1)}, bf16[4,64,128]{2,1,0:T(8,128)(2,1)S(1)}, u32[]{:S(2)}, u32[]{:S(2)}) collective-permute-start(bf16[4,64,128]{2,1,0:T(8,128)(2,1)} %get-tuple-element.62), channel_id=1, source_target_pairs={{0,16},{16,0},{1,17},{17,1},{2,18},{18,2},{3,19},{19,3},{4,20},{20... | collective-permute-start | bytes 196616 | tf_op jit(solution)/shard_map/ppermute | solution.py:442
  80.3 9.8 %collective-permute-start.14 = (bf16[4,64,128]{2,1,0:T(8,128)(2,1)}, bf16[4,64,128]{2,1,0:T(8,128)(2,1)S(1)}, u32[]{:S(2)}, u32[]{:S(2)}) collective-permute-start(bf16[4,64,128]{2,1,0:T(8,128)(2,1)} %get-tuple-element.63), channel_id=1, source_target_pairs={{0,18},{2,16},{4,22},{6,20},{8,26},{10,24},{12,30},{14,28},{16,2},... | collective-permute-start | bytes 196616 | tf_op jit(solution)/shard_map/ppermute | solution.py:444
  95.3 17.6 %collective-permute-start.15 = (f32[384,128]{1,0:T(8,128)}, f32[384,128]{1,0:T(8,128)S(1)}, u32[]{:S(2)}, u32[]{:S(2)}) collective-permute-start(f32[384,128]{1,0:T(8,128)} %get-tuple-element.69), channel_id=1, source_target_pairs={{0,2},{2,0},{4,6},{6,4},{8,10},{10,8},{12,14},{14,12},{1,3},{3,1},... | collective-permute-start | bytes 589832 | tf_op jit(solution)/shard_map/ppermute | solution.py:443
  95.9 16.9 %collective-permute-start.16 = (f32[384,128]{1,0:T(8,128)}, f32[384,128]{1,0:T(8,128)S(1)}, u32[]{:S(2)}, u32[]{:S(2)}) collective-permute-start(f32[384,128]{1,0:T(8,128)} %get-tuple-element.74), channel_id=1, source_target_pairs={{0,16},{16,0},{1,17},{17,1},{2,18},{18,2},{3,19},{19,3},{4,20},{20... | collective-permute-start | bytes 589832 | tf_op jit(solution)/shard_map/ppermute | solution.py:442
  97.2 15.6 %collective-permute-start.17 = (f32[384,128]{1,0:T(8,128)}, f32[384,128]{1,0:T(8,128)S(1)}, u32[]{:S(2)}, u32[]{:S(2)}) collective-permute-start(f32[384,128]{1,0:T(8,128)} %get-tuple-element.76), channel_id=1, source_target_pairs={{0,18},{2,16},{4,22},{6,20},{8,26},{10,24},{12,30},{14,28},{16,2},... | collective-permute-start | bytes 589832 | tf_op jit(solution)/shard_map/ppermute | solution.py:444
  98.3 14.5 %copy-start.9 = (f32[384,128]{1,0:T(8,128)S(1)}, f32[384,128]{1,0:T(8,128)}, u32[]{:S(2)}) copy-start(f32[384,128]{1,0:T(8,128)} %get-tuple-element.68) | copy-start | bytes 589828
  112.8 6.8 %copy-start.2 = (bf16[384,2048]{1,0:T(8,128)(2,1)S(1)}, bf16[384,2048]{1,0:T(8,128)(2,1)}, u32[]{:S(2)}) copy-start(bf16[384,2048]{1,0:T(8,128)(2,1)} %q_ref.4) | copy-start | bytes 4718596
  112.8 6.8 %copy-start.3 = (f32[2,2,384,128]{3,2,1,0:T(8,128)S(1)}, f32[2,2,384,128]{3,2,1,0:T(8,128)}, u32[]{:S(2)}) copy-start(f32[2,2,384,128]{3,2,1,0:T(8,128)} %get-tuple-element.78.stat_ref) | copy-start | bytes 2359300
  112.8 6.8 %copy-start.4 = (bf16[4,64,128]{2,1,0:T(8,128)(2,1)S(1)}, bf16[4,64,128]{2,1,0:T(8,128)(2,1)}, u32[]{:S(2)}) copy-start(bf16[4,64,128]{2,1,0:T(8,128)(2,1)} %get-tuple-element.60.up0) | copy-start | bytes 196612
  112.8 6.8 %copy-start.5 = (s32[4,4]{1,0:T(4,128)S(1)}, s32[4,4]{1,0:T(4,128)}, u32[]{:S(2)}) copy-start(s32[4,4]{1,0:T(4,128)} %pad_add_fusion.info) | copy-start | bytes 196
  112.9 6.7 %collective-permute-start.18 = (f32[384,128]{1,0:T(8,128)S(1)}, f32[384,128]{1,0:T(8,128)S(1)}, u32[]{:S(2)}, u32[]{:S(2)}) collective-permute-start(f32[384,128]{1,0:T(8,128)S(1)} %add_add_fusion.mine_ref), channel_id=1, source_target_pairs={{0,1},{1,0},{2,3},{3,2},{4,5},{5,4},{6,7},{7,6},{8,9},{9,8},{10,11... | collective-permute-start | bytes 589832 | tf_op jit(solution)/shard_map/ppermute | solution.py:538
  (2 other events, 3.5 us)

commit v3 on v2

--- a/solution.py
+++ b/solution.py
@@ -17,7 +17,7 @@
 LOG2E = 1.4426950408889634
 NEG = -1e30
 TILE = 32
-CHUNK = 512
+CHUNK = 256
 PART = 8
 ALIGN = 16
 VMEM = 60 * 1024 * 1024

time: 131 us -> 130 us (level)
  the two profiles are of different devices: /device:TPU:17 before, /device:TPU:0 now
where the time goes in v3:
time: 130 us; the launch traced here: 128 us
  Pallas kernels  50.4 us (39%)
  starting transfers between devices  29 us (22%)
  waiting for transfers between devices  16.9 us (13%)
  other arithmetic  12.3 us (9%)
  matrix products  11.6 us (9%)
  local copies, waits for them, and re-layouts  7.16 us (6%)
    pallas_call x3, Pallas kernels, cached_attention(): pl.pallas_call(functools.partial(cached_kernel, first, carry_on), grid_sp...  30.5 us
    ppermute x8, starting transfers between devices, body(): lax.ppermute(a, 'replica', [(2 * f + p, 2 * t + p) for f, t in pairs for...  14.3 us
    pallas_call x2, Pallas kernels, low_rank_step(): pl.pallas_call(functools.partial(low_rank_kernel, pick, len(pieces)), in_...  11 us
    ppermute x4, waiting for transfers between devices, body(): lax.ppermute(a, 'replica', [(r, r ^ 1) for r in range(n_replica)])  9.46 us
    pallas_call x1, Pallas kernels, final_step(): pl.pallas_call(final_kernel, grid_spec=pltpu.PrefetchScalarGridSpec(num_s...  8.83 us
    ppermute x8, waiting for transfers between devices, body(): lax.ppermute(a, 'replica', [(2 * f + p, 2 * t + p) for f, t in pairs for...  6.95 us
    ppermute x3, starting transfers between devices, body(): by_x = lambda a: lax.ppermute(a, 'groups', [(0, 1), (1, 0)])  6.29 us
    dot_general x1, matrix products, body(): jnp.dot(tokens_later, key_weight_matrix, preferred_element_type=jnp.float32)  5.8 us
  transfers between devices with their start and end apart: 19, of which 5 were waited for; matrix products, arithmetic and copies ran while one was open for 20% of the time, Pallas kernels for 29%

profile of v3, /device:TPU:0, one launch (start us, length us, event | category | flops | bytes accessed | tf_op | source)
XLA Modules:
  0.0 128.4 jit_solution(5143313373339969857)
XLA Ops:
  0.7 1.5 %copy-done = bf16[2,4096,128]{2,1,0:T(8,128)(2,1)S(1)} copy-done((bf16[2,4096,128]{2,1,0:T(8,128)(2,1)S(1)}, bf16[2,4096,128]{2,1,0:T(8,128)(2,1)}, u32[]{:S(2)}) %copy-start) | copy-done | bytes 2097176
  4.0 3.0 %collective-permute-start = (bf16[2,1088,128]{2,1,0:T(8,128)(2,1)}, bf16[2,1088,128]{2,1,0:T(8,128)(2,1)}, u32[]{:S(2)}, u32[]{:S(2)}) collective-permute-start(bf16[2,1088,128]{2,1,0:T(8,128)(2,1)} %pad_maximum_fusion.5), channel_id=1, source_target_pairs={{0,2},{2,0},{4,6},{6,4},{8,10},{10,8},{12,14},{14,12},{1,3},{3,1},... | collective-permute-start | bytes 1671176 | tf_op jit(solution)/shard_map/ppermute | solution.py:443
  7.0 0.9 pad_maximum_fusion.6.refs_4_
  7.8 1.6 %collective-permute-start.7 = (bf16[2,1088,128]{2,1,0:T(8,128)(2,1)}, bf16[2,1088,128]{2,1,0:T(8,128)(2,1)}, u32[]{:S(2)}, u32[]{:S(2)}) collective-permute-start(bf16[2,1088,128]{2,1,0:T(8,128)(2,1)} %pad_maximum_fusion.6.refs_4_), channel_id=1, source_target_pairs={{0,4},{2,6},{4,0},{6,2},{8,12},{10,14},{12,8},{14,10},{1,5},{3,7},... | collective-permute-start | bytes 1671176 | tf_op jit(solution)/shard_map/ppermute | solution.py:453
  9.4 1.5 %collective-permute-start.10 = (bf16[2,1088,128]{2,1,0:T(8,128)(2,1)}, bf16[2,1088,128]{2,1,0:T(8,128)(2,1)}, u32[]{:S(2)}, u32[]{:S(2)}) collective-permute-start(bf16[2,1088,128]{2,1,0:T(8,128)(2,1)} %pad_maximum_fusion.6.refs_4_), channel_id=1, source_target_pairs={{4,8},{6,10},{8,4},{10,6},{5,9},{7,11},{9,5},{11,7},{20,24},{22,26... | collective-permute-start | bytes 1671176 | tf_op jit(solution)/shard_map/ppermute | solution.py:453
  11.4 1.8 %constant_dynamic-slice_fusion.1 = (bf16[384,1024]{1,0:T(8,128)(2,1)S(1)}, bf16[384,1024]{1,0:T(8,128)(2,1)S(1)}, bf16[384,1024]{1,0:T(8,128)(2,1)S(1)}) fusion(bf16[384,8192]{1,0:T(8,128)(2,1)} %refs_0_.3, s32[]{:T(128)S(6)} %select_n.82, s32[]{:T(128)S(6)} %select_n.81, s32[]{:T(128)S(6)} %select_n.80), kind=kLoop, calls=%fused_computation.38 | loop fusion | bytes 4718604 | tf_op jit(solution)/shard_map/dynamic_slice | solution.py:477
  13.2 1.5 %pad_maximum_fusion = (bf16[400,1024]{1,0:T(8,128)(2,1)}, bf16[400,1024]{1,0:T(8,128)(2,1)}, bf16[400,1024]{1,0:T(8,128)(2,1)}) fusion(bf16[16,1024]{1,0:T(8,128)(2,1)S(1)} %fusion.6, bf16[384,1024]{1,0:T(8,128)(2,1)S(1)} %get-tuple-element.79, bf16[384,1024]{1,0:T(8,128)(2,1)S(1)} %get-tuple-element.80, bf16[384,1024]{1,0:T(8,128)(2,1)S(1)} %get-tuple-element.81), kind=kLoop, calls=%fused_computation | loop fusion | flops 4096000 | bytes 4849664 | tf_op jit(solution)/shard_map/concatenate | solution.py:476
  14.7 1.5 %collective-permute-start.2 = (bf16[400,1024]{1,0:T(8,128)(2,1)}, bf16[400,1024]{1,0:T(8,128)(2,1)S(1)}, u32[]{:S(2)}, u32[]{:S(2)}) collective-permute-start(bf16[400,1024]{1,0:T(8,128)(2,1)} %get-tuple-element.86), channel_id=1, source_target_pairs={{0,16},{16,0},{1,17},{17,1},{2,18},{18,2},{3,19},{19,3},{4,20},{20... | collective-permute-start | bytes 2457608 | tf_op jit(solution)/shard_map/ppermute | solution.py:442
  17.8 2.0 %collective-permute-done.refs_5_ = bf16[2,1088,128]{2,1,0:T(8,128)(2,1)} collective-permute-done((bf16[2,1088,128]{2,1,0:T(8,128)(2,1)}, bf16[2,1088,128]{2,1,0:T(8,128)(2,1)}, u32[]{:S(2)}, u32[]{:S(2)}) %collective-permute-start) | collective-permute-done | bytes 557088 | tf_op jit(solution)/shard_map/ppermute | solution.py:443
  19.9 1.8 %collective-permute-start.4 = (bf16[2,1088,128]{2,1,0:T(8,128)(2,1)}, bf16[2,1088,128]{2,1,0:T(8,128)(2,1)S(1)}, u32[]{:S(2)}, u32[]{:S(2)}) collective-permute-start(bf16[2,1088,128]{2,1,0:T(8,128)(2,1)} %collective-permute-done.refs_5_), channel_id=1, source_target_pairs={{0,4},{2,6},{4,0},{6,2},{8,12},{10,14},{12,8},{14,10},{1,5},{3,7},... | collective-permute-start | bytes 1671176 | tf_op jit(solution)/shard_map/ppermute | solution.py:453
  22.4 5.8 %fusion.9.pk_ref = f32[384,256]{1,0:T(8,128)S(1)} fusion(bf16[384,8192]{1,0:T(8,128)(2,1)} %refs_0_.3, bf16[8192,256]{1,0:T(8,128)(2,1)} %param.16), kind=kOutput, calls=%fused_computation.54 | convolution fusion | flops 1610612736 | bytes 10878976 | tf_op jit(solution)/shard_map/dot_general | solution.py:488
  29.0 4.4 %collective-permute-start.6 = (bf16[2,2,64,128]{3,2,1,0:T(8,128)(2,1)S(1)}, bf16[2,2,64,128]{3,2,1,0:T(8,128)(2,1)S(1)}, u32[]{:S(2)}, u32[]{:S(2)}) collective-permute-start(bf16[2,2,64,128]{3,2,1,0:T(8,128)(2,1)S(1)} %pad_maximum_fusion.9), channel_id=1, source_target_pairs={{0,12},{2,14},{12,0},{14,2},{1,13},{3,15},{13,1},{15,3},{16,28},{1... | collective-permute-start | bytes 196616 | tf_op jit(solution)/shard_map/ppermute | solution.py:453
  34.1 1.3 collective-permute-start.1
  35.3 2.1 %pad_maximum_fusion.3 = bf16[2,2,1088,128]{3,2,1,0:T(8,128)(2,1)} fusion(bf16[1,2,1088,128]{3,2,1,0:T(8,128)(2,1)S(1)} %bitcast.28, bf16[1,2,1088,128]{3,2,1,0:T(8,128)(2,1)} %bitcast.11), kind=kLoop, calls=%fused_computation.3 | loop fusion | flops 557056 | bytes 2228224 | tf_op jit(solution)/shard_map/stack | solution.py:492
  37.5 1.7 %collective-permute-start.3 = (bf16[400,1024]{1,0:T(8,128)(2,1)}, bf16[400,1024]{1,0:T(8,128)(2,1)}, u32[]{:S(2)}, u32[]{:S(2)}) collective-permute-start(bf16[400,1024]{1,0:T(8,128)(2,1)} %get-tuple-element.42), channel_id=1, source_target_pairs={{0,18},{2,16},{4,22},{6,20},{8,26},{10,24},{12,30},{14,28},{16,2},... | collective-permute-start | bytes 2457608 | tf_op jit(solution)/shard_map/ppermute | solution.py:444
  39.2 1.7 %collective-permute-start.8 = (bf16[2,2,1088,128]{3,2,1,0:T(8,128)(2,1)}, bf16[2,2,1088,128]{3,2,1,0:T(8,128)(2,1)}, u32[]{:S(2)}, u32[]{:S(2)}) collective-permute-start(bf16[2,2,1088,128]{3,2,1,0:T(8,128)(2,1)} %pad_maximum_fusion.3), channel_id=1, source_target_pairs={{4,8},{6,10},{8,4},{10,6},{5,9},{7,11},{9,5},{11,7},{20,24},{22,26... | collective-permute-start | bytes 3342344 | tf_op jit(solution)/shard_map/ppermute | solution.py:453
  40.8 2.2 %pad_maximum_fusion.4 = bf16[2,2,1088,128]{3,2,1,0:T(8,128)(2,1)} fusion(bf16[1,2,1088,128]{3,2,1,0:T(8,128)(2,1)S(1)} %bitcast.29, bf16[1,2,1088,128]{3,2,1,0:T(8,128)(2,1)} %bitcast.13), kind=kLoop, calls=%fused_computation.4 | loop fusion | flops 557056 | bytes 2228224 | tf_op jit(solution)/shard_map/stack | solution.py:494
  43.0 1.3 %collective-permute-start.11 = (bf16[2,2,1088,128]{3,2,1,0:T(8,128)(2,1)}, bf16[2,2,1088,128]{3,2,1,0:T(8,128)(2,1)}, u32[]{:S(2)}, u32[]{:S(2)}) collective-permute-start(bf16[2,2,1088,128]{3,2,1,0:T(8,128)(2,1)} %pad_maximum_fusion.4), channel_id=1, source_target_pairs={{4,0},{6,2},{8,12},{10,14},{5,1},{7,3},{9,13},{11,15},{20,16},{22,... | collective-permute-start | bytes 3342344 | tf_op jit(solution)/shard_map/ppermute | solution.py:453
  44.3 13.1 %cached_attention.3 = (f32[2,384,1024]{2,1,0:T(8,128)}, f32[2,2,384,128]{3,2,1,0:T(8,128)}) custom-call(s32[4,4]{1,0:T(4,128)} %pad_add_fusion.info, bf16[384,2048]{1,0:T(8,128)(2,1)} %q_ref.4, bf16[4,2048,256]{2,1,0:T(8,128)(2,1)} %k_ref.5, bf16[4,2048,256]{2,1,0:T(8,128)(2,1)} %v_ref.5), custom_call_target="tpu_custom_call" | custom-call | flops 6442450944 | bytes 6291456 | tf_op jit(solution)/shard_map/cached_attention/pallas_call | solution.py:116
  57.4 5.8 %fusion.10.pv_ref = f32[384,256]{1,0:T(8,128)S(1)} fusion(bf16[384,8192]{1,0:T(8,128)(2,1)} %refs_0_.3, bf16[8192,256]{1,0:T(8,128)(2,1)} %param.17), kind=kOutput, calls=%fused_computation.55 | convolution fusion | flops 1610612736 | bytes 10878976 | tf_op jit(solution)/shard_map/dot_general | solution.py:497
  63.2 7.4 %collective-permute-done.1.refs_1_ = bf16[400,1024]{1,0:T(8,128)(2,1)} collective-permute-done((bf16[400,1024]{1,0:T(8,128)(2,1)}, bf16[400,1024]{1,0:T(8,128)(2,1)}, u32[]{:S(2)}, u32[]{:S(2)}) %collective-permute-start.1) | collective-permute-done | bytes 819232 | tf_op jit(solution)/shard_map/ppermute | solution.py:443
  71.3 1.5 %collective-permute-start.9 = (bf16[2,2,1088,128]{3,2,1,0:T(8,128)(2,1)}, bf16[2,2,1088,128]{3,2,1,0:T(8,128)(2,1)}, u32[]{:S(2)}, u32[]{:S(2)}) collective-permute-start(bf16[2,2,1088,128]{3,2,1,0:T(8,128)(2,1)} %collective-permute-done.8.refs_10_), channel_id=1, source_target_pairs={{4,0},{6,2},{8,12},{10,14},{5,1},{7,3},{9,13},{11,15},{20,16},{22,... | collective-permute-start | bytes 3342344 | tf_op jit(solution)/shard_map/ppermute | solution.py:453
  74.1 6.5 %low_rank_early.1 = (f32[384,128]{1,0:T(8,128)}, f32[384,128]{1,0:T(8,128)}, f32[384,128]{1,0:T(8,128)}, f32[384,128]{1,0:T(8,128)}, bf16[4,64,128]{2,1,0:T(8,12...) custom-call(s32[3]{0:T(128)} %pad_add_fusion.2.place, ...), custom_call_target="tpu_custom_call" | custom-call | flops 1610612736 | bytes 6291456 | tf_op jit(solution)/shard_map/low_rank_early/pallas_call | solution.py:235
  81.5 1.5 %collective-permute-start.13 = (bf16[4,64,128]{2,1,0:T(8,128)(2,1)}, bf16[4,64,128]{2,1,0:T(8,128)(2,1)S(1)}, u32[]{:S(2)}, u32[]{:S(2)}) collective-permute-start(bf16[4,64,128]{2,1,0:T(8,128)(2,1)} %get-tuple-element.62), channel_id=1, source_target_pairs={{0,16},{16,0},{1,17},{17,1},{2,18},{18,2},{3,19},{19,3},{4,20},{20... | collective-permute-start | bytes 196616 | tf_op jit(solution)/shard_map/ppermute | solution.py:442
  82.9 1.2 collective-permute-start.14
  84.2 7.2 %cached_attention.4 = (f32[2,384,1024]{2,1,0:T(8,128)}, f32[2,2,384,128]{3,2,1,0:T(8,128)}) custom-call(s32[4,4]{1,0:T(4,128)} %pad_add_fusion.info, bf16[384,2048]{1,0:T(8,128)(2,1)} %q_ref.4, bf16[4,2048,256]{2,1,0:T(8,128)(2,1)} %k_ref.5, bf16[4,2048,256]{2,1,0:T(8,128)(2,1)} %v_ref.5, ...), custom_call_target="tpu_custom_call", output_to_operand_aliasing={{0}: (4, {}), {1}: (5, {})} | custom-call | flops 6442450944 | bytes 6291456 | tf_op jit(solution)/shard_map/cached_attention/pallas_call | solution.py:116
  91.4 6.2 %collective-permute-done.9.refs_4_ = bf16[2,2,1088,128]{3,2,1,0:T(8,128)(2,1)} collective-permute-done((bf16[2,2,1088,128]{3,2,1,0:T(8,128)(2,1)}, bf16[2,2,1088,128]{3,2,1,0:T(8,128)(2,1)}, u32[]{:S(2)}, u32[]{:S(2)}) %collective-permute-start.9) | collective-permute-done | bytes 1114144 | tf_op jit(solution)/shard_map/ppermute | solution.py:453
  97.6 4.5 %low_rank_late.1 = (f32[384,128]{1,0:T(8,128)}, f32[384,128]{1,0:T(8,128)}, f32[384,128]{1,0:T(8,128)}, f32[384,128]{1,0:T(8,128)}) custom-call(s32[3]{0:T(128)} %pad_add_fusion.2.place, s32[4,8]{1,0:T(4,128)} %pad_add_fusion.1.infos, bf16[384,8192]{1,0:T(8,128)(2,1)} %refs_0_.3, bf16[400,1024]{1,0:T(8,128)(2,1)} %collective-permute-done.1.refs_1_, ...), custom_call_target="tpu_custom_call" | custom-call | flops 1610612736 | bytes 6291456 | tf_op jit(solution)/shard_map/low_rank_late/pallas_call | solution.py:235
  102.5 3.3 %collective-permute-start.16 = (f32[384,128]{1,0:T(8,128)}, f32[384,128]{1,0:T(8,128)S(1)}, u32[]{:S(2)}, u32[]{:S(2)}) collective-permute-start(f32[384,128]{1,0:T(8,128)} %get-tuple-element.74), channel_id=1, source_target_pairs={{0,16},{16,0},{1,17},{17,1},{2,18},{18,2},{3,19},{19,3},{4,20},{20... | collective-permute-start | bytes 589832 | tf_op jit(solution)/shard_map/ppermute | solution.py:442
  105.8 10.3 %cached_attention.5 = (f32[2,384,1024]{2,1,0:T(8,128)}, f32[2,2,384,128]{3,2,1,0:T(8,128)}) custom-call(s32[4,4]{1,0:T(4,128)} %pad_add_fusion.info, bf16[384,2048]{1,0:T(8,128)(2,1)} %q_ref.4, bf16[4,2048,256]{2,1,0:T(8,128)(2,1)} %k_ref.5, bf16[4,2048,256]{2,1,0:T(8,128)(2,1)} %v_ref.5, ...), custom_call_target="tpu_custom_call", output_to_operand_aliasing={{0}: (4, {}), {1}: (5, {})} | custom-call | flops 6442450944 | bytes 6291456 | tf_op jit(solution)/shard_map/cached_attention/pallas_call | solution.py:116
  117.7 1.9 %copy-done.1 = f32[2,384,1024]{2,1,0:T(8,128)S(1)} copy-done((f32[2,384,1024]{2,1,0:T(8,128)S(1)}, f32[2,384,1024]{2,1,0:T(8,128)}, u32[]{:S(2)}) %copy-start.1) | copy-done | bytes 3145752
  119.6 8.8 %final_step.1 = (bf16[384,2048]{1,0:T(8,128)(2,1)}, bf16[384,256]{1,0:T(8,128)(2,1)}, bf16[384,256]{1,0:T(8,128)(2,1)}) custom-call(s32[4,4]{1,0:T(4,128)S(1)} %copy-done.5, f32[384,128]{1,0:T(8,128)S(1)} %add_add_fusion.mine_ref, f32[384,128]{1,0:T(8,128)S(1)} %collective-permute-done.18.other_ref, f32[384,256]{1,0:T(8,128)S(1)} %fusion.9.pk_ref, ...), custom_call_target="tpu_custom_call" | custom-call | tf_op jit(solution)/shard_map/final_step/pallas_call | solution.py:351
  (80 shorter events, 10.8 us)
Async XLA Ops:
  3.1 7.8 %copy-start.11 = (s32[8,4]{0,1:T(4,128)S(1)}, s32[8,4]{0,1:T(4,128)}, u32[]{:S(2)}) copy-start(s32[8,4]{0,1:T(4,128)} %param.21) | copy-start | bytes 388
  3.1 8.0 %copy-start.14 = (s32[16]{0:T(128)S(1)}, s32[16]{0:T(128)}, u32[]{:S(2)}) copy-start(s32[16]{0:T(128)} %param.20) | copy-start | bytes 196
  3.1 8.2 %copy-start.12 = (s32[1,4]{1,0:T(1,128)S(1)}, s32[1,4]{1,0:T(1,128)}, u32[]{:S(2)}) copy-start(s32[1,4]{1,0:T(1,128)} %param.22) | copy-start | bytes 52
  4.0 15.9 %collective-permute-start = (bf16[2,1088,128]{2,1,0:T(8,128)(2,1)}, bf16[2,1088,128]{2,1,0:T(8,128)(2,1)}, u32[]{:S(2)}, u32[]{:S(2)}) collective-permute-start(bf16[2,1088,128]{2,1,0:T(8,128)(2,1)} %pad_maximum_fusion.5), channel_id=1, source_target_pairs={{0,2},{2,0},{4,6},{6,4},{8,10},{10,8},{12,14},{14,12},{1,3},{3,1},... | collective-permute-start | bytes 1671176 | tf_op jit(solution)/shard_map/ppermute | solution.py:443
  7.8 21.1 %collective-permute-start.7 = (bf16[2,1088,128]{2,1,0:T(8,128)(2,1)}, bf16[2,1088,128]{2,1,0:T(8,128)(2,1)}, u32[]{:S(2)}, u32[]{:S(2)}) collective-permute-start(bf16[2,1088,128]{2,1,0:T(8,128)(2,1)} %pad_maximum_fusion.6.refs_4_), channel_id=1, source_target_pairs={{0,4},{2,6},{4,0},{6,2},{8,12},{10,14},{12,8},{14,10},{1,5},{3,7},... | collective-permute-start | bytes 1671176 | tf_op jit(solution)/shard_map/ppermute | solution.py:453
  9.4 28.1 %collective-permute-start.10 = (bf16[2,1088,128]{2,1,0:T(8,128)(2,1)}, bf16[2,1088,128]{2,1,0:T(8,128)(2,1)}, u32[]{:S(2)}, u32[]{:S(2)}) collective-permute-start(bf16[2,1088,128]{2,1,0:T(8,128)(2,1)} %pad_maximum_fusion.6.refs_4_), channel_id=1, source_target_pairs={{4,8},{6,10},{8,4},{10,6},{5,9},{7,11},{9,5},{11,7},{20,24},{22,26... | collective-permute-start | bytes 1671176 | tf_op jit(solution)/shard_map/ppermute | solution.py:453
  13.2 3.4 %copy-start.13 = (s32[1,4]{1,0:T(1,128)S(1)}, s32[1,4]{1,0:T(1,128)}, u32[]{:S(2)}) copy-start(s32[1,4]{1,0:T(1,128)} %param.23) | copy-start | bytes 52
  14.7 29.6 %collective-permute-start.2 = (bf16[400,1024]{1,0:T(8,128)(2,1)}, bf16[400,1024]{1,0:T(8,128)(2,1)S(1)}, u32[]{:S(2)}, u32[]{:S(2)}) collective-permute-start(bf16[400,1024]{1,0:T(8,128)(2,1)} %get-tuple-element.86), channel_id=1, source_target_pairs={{0,16},{16,0},{1,17},{17,1},{2,18},{18,2},{3,19},{19,3},{4,20},{20... | collective-permute-start | bytes 2457608 | tf_op jit(solution)/shard_map/ppermute | solution.py:442
  19.9 14.2 %collective-permute-start.4 = (bf16[2,1088,128]{2,1,0:T(8,128)(2,1)}, bf16[2,1088,128]{2,1,0:T(8,128)(2,1)S(1)}, u32[]{:S(2)}, u32[]{:S(2)}) collective-permute-start(bf16[2,1088,128]{2,1,0:T(8,128)(2,1)} %collective-permute-done.refs_5_), channel_id=1, source_target_pairs={{0,4},{2,6},{4,0},{6,2},{8,12},{10,14},{12,8},{14,10},{1,5},{3,7},... | collective-permute-start | bytes 1671176 | tf_op jit(solution)/shard_map/ppermute | solution.py:453
  21.7 17.5 %collective-permute-start.5 = (bf16[2,1088,128]{2,1,0:T(8,128)(2,1)}, bf16[2,1088,128]{2,1,0:T(8,128)(2,1)S(1)}, u32[]{:S(2)}, u32[]{:S(2)}) collective-permute-start(bf16[2,1088,128]{2,1,0:T(8,128)(2,1)} %collective-permute-done.refs_5_), channel_id=1, source_target_pairs={{4,8},{6,10},{8,4},{10,6},{5,9},{7,11},{9,5},{11,7},{20,24},{22,26... | collective-permute-start | bytes 1671176 | tf_op jit(solution)/shard_map/ppermute | solution.py:453
  29.0 14.0 %collective-permute-start.6 = (bf16[2,2,64,128]{3,2,1,0:T(8,128)(2,1)S(1)}, bf16[2,2,64,128]{3,2,1,0:T(8,128)(2,1)S(1)}, u32[]{:S(2)}, u32[]{:S(2)}) collective-permute-start(bf16[2,2,64,128]{3,2,1,0:T(8,128)(2,1)S(1)} %pad_maximum_fusion.9), channel_id=1, source_target_pairs={{0,12},{2,14},{12,0},{14,2},{1,13},{3,15},{13,1},{15,3},{16,28},{1... | collective-permute-start | bytes 196616 | tf_op jit(solution)/shard_map/ppermute | solution.py:453
  34.1 8.9 %copy-start.7 = (bf16[2,1088,128]{2,1,0:T(8,128)(2,1)}, bf16[2,1088,128]{2,1,0:T(8,128)(2,1)S(1)}, u32[]{:S(2)}) copy-start(bf16[2,1088,128]{2,1,0:T(8,128)(2,1)S(1)} %collective-permute-done.4.refs_7_) | copy-start | bytes 1671172
  34.1 36.5 %collective-permute-start.1 = (bf16[400,1024]{1,0:T(8,128)(2,1)}, bf16[400,1024]{1,0:T(8,128)(2,1)}, u32[]{:S(2)}, u32[]{:S(2)}) collective-permute-start(bf16[400,1024]{1,0:T(8,128)(2,1)} %get-tuple-element.41), channel_id=1, source_target_pairs={{0,2},{2,0},{4,6},{6,4},{8,10},{10,8},{12,14},{14,12},{1,3},{3,1},... | collective-permute-start | bytes 2457608 | tf_op jit(solution)/shard_map/ppermute | solution.py:443
  37.5 33.1 %collective-permute-start.3 = (bf16[400,1024]{1,0:T(8,128)(2,1)}, bf16[400,1024]{1,0:T(8,128)(2,1)}, u32[]{:S(2)}, u32[]{:S(2)}) collective-permute-start(bf16[400,1024]{1,0:T(8,128)(2,1)} %get-tuple-element.42), channel_id=1, source_target_pairs={{0,18},{2,16},{4,22},{6,20},{8,26},{10,24},{12,30},{14,28},{16,2},... | collective-permute-start | bytes 2457608 | tf_op jit(solution)/shard_map/ppermute | solution.py:444
  39.2 3.8 %copy-start.8 = (bf16[2,1088,128]{2,1,0:T(8,128)(2,1)}, bf16[2,1088,128]{2,1,0:T(8,128)(2,1)S(1)}, u32[]{:S(2)}) copy-start(bf16[2,1088,128]{2,1,0:T(8,128)(2,1)S(1)} %collective-permute-done.5.refs_9_) | copy-start | bytes 1671172
  39.2 32.1 %collective-permute-start.8 = (bf16[2,2,1088,128]{3,2,1,0:T(8,128)(2,1)}, bf16[2,2,1088,128]{3,2,1,0:T(8,128)(2,1)}, u32[]{:S(2)}, u32[]{:S(2)}) collective-permute-start(bf16[2,2,1088,128]{3,2,1,0:T(8,128)(2,1)} %pad_maximum_fusion.3), channel_id=1, source_target_pairs={{4,8},{6,10},{8,4},{10,6},{5,9},{7,11},{9,5},{11,7},{20,24},{22,26... | collective-permute-start | bytes 3342344 | tf_op jit(solution)/shard_map/ppermute | solution.py:453
  43.0 14.4 %copy-start.10 = (bf16[2,2,64,128]{3,2,1,0:T(8,128)(2,1)}, bf16[2,2,64,128]{3,2,1,0:T(8,128)(2,1)S(1)}, u32[]{:S(2)}) copy-start(bf16[2,2,64,128]{3,2,1,0:T(8,128)(2,1)S(1)} %collective-permute-done.6.refs_12_) | copy-start | bytes 196612
  43.0 31.1 %collective-permute-start.11 = (bf16[2,2,1088,128]{3,2,1,0:T(8,128)(2,1)}, bf16[2,2,1088,128]{3,2,1,0:T(8,128)(2,1)}, u32[]{:S(2)}, u32[]{:S(2)}) collective-permute-start(bf16[2,2,1088,128]{3,2,1,0:T(8,128)(2,1)} %pad_maximum_fusion.4), channel_id=1, source_target_pairs={{4,0},{6,2},{8,12},{10,14},{5,1},{7,3},{9,13},{11,15},{20,16},{22,... | collective-permute-start | bytes 3342344 | tf_op jit(solution)/shard_map/ppermute | solution.py:453
  44.3 28.5 %copy-start.6 = (bf16[400,1024]{1,0:T(8,128)(2,1)}, bf16[400,1024]{1,0:T(8,128)(2,1)S(1)}, u32[]{:S(2)}) copy-start(bf16[400,1024]{1,0:T(8,128)(2,1)S(1)} %collective-permute-done.2.refs_2_) | copy-start | bytes 2457604
  71.3 26.3 %collective-permute-start.9 = (bf16[2,2,1088,128]{3,2,1,0:T(8,128)(2,1)}, bf16[2,2,1088,128]{3,2,1,0:T(8,128)(2,1)}, u32[]{:S(2)}, u32[]{:S(2)}) collective-permute-start(bf16[2,2,1088,128]{3,2,1,0:T(8,128)(2,1)} %collective-permute-done.8.refs_10_), channel_id=1, source_target_pairs={{4,0},{6,2},{8,12},{10,14},{5,1},{7,3},{9,13},{11,15},{20,16},{22,... | collective-permute-start | bytes 3342344 | tf_op jit(solution)/shard_map/ppermute | solution.py:453
  80.6 10.7 %collective-permute-start.12 = (bf16[4,64,128]{2,1,0:T(8,128)(2,1)}, bf16[4,64,128]{2,1,0:T(8,128)(2,1)S(1)}, u32[]{:S(2)}, u32[]{:S(2)}) collective-permute-start(bf16[4,64,128]{2,1,0:T(8,128)(2,1)} %get-tuple-element.61), channel_id=1, source_target_pairs={{0,2},{2,0},{4,6},{6,4},{8,10},{10,8},{12,14},{14,12},{1,3},{3,1},... | collective-permute-start | bytes 196616 | tf_op jit(solution)/shard_map/ppermute | solution.py:443
  81.5 9.9 %collective-permute-start.13 = (bf16[4,64,128]{2,1,0:T(8,128)(2,1)}, bf16[4,64,128]{2,1,0:T(8,128)(2,1)S(1)}, u32[]{:S(2)}, u32[]{:S(2)}) collective-permute-start(bf16[4,64,128]{2,1,0:T(8,128)(2,1)} %get-tuple-element.62), channel_id=1, source_target_pairs={{0,16},{16,0},{1,17},{17,1},{2,18},{18,2},{3,19},{19,3},{4,20},{20... | collective-permute-start | bytes 196616 | tf_op jit(solution)/shard_map/ppermute | solution.py:442
  82.9 8.4 %collective-permute-start.14 = (bf16[4,64,128]{2,1,0:T(8,128)(2,1)}, bf16[4,64,128]{2,1,0:T(8,128)(2,1)S(1)}, u32[]{:S(2)}, u32[]{:S(2)}) collective-permute-start(bf16[4,64,128]{2,1,0:T(8,128)(2,1)} %get-tuple-element.63), channel_id=1, source_target_pairs={{0,18},{2,16},{4,22},{6,20},{8,26},{10,24},{12,30},{14,28},{16,2},... | collective-permute-start | bytes 196616 | tf_op jit(solution)/shard_map/ppermute | solution.py:444
  102.1 13.9 %collective-permute-start.15 = (f32[384,128]{1,0:T(8,128)}, f32[384,128]{1,0:T(8,128)S(1)}, u32[]{:S(2)}, u32[]{:S(2)}) collective-permute-start(f32[384,128]{1,0:T(8,128)} %get-tuple-element.69), channel_id=1, source_target_pairs={{0,2},{2,0},{4,6},{6,4},{8,10},{10,8},{12,14},{14,12},{1,3},{3,1},... | collective-permute-start | bytes 589832 | tf_op jit(solution)/shard_map/ppermute | solution.py:443
  102.5 13.6 %collective-permute-start.16 = (f32[384,128]{1,0:T(8,128)}, f32[384,128]{1,0:T(8,128)S(1)}, u32[]{:S(2)}, u32[]{:S(2)}) collective-permute-start(f32[384,128]{1,0:T(8,128)} %get-tuple-element.74), channel_id=1, source_target_pairs={{0,16},{16,0},{1,17},{17,1},{2,18},{18,2},{3,19},{19,3},{4,20},{20... | collective-permute-start | bytes 589832 | tf_op jit(solution)/shard_map/ppermute | solution.py:442
  105.8 10.3 %collective-permute-start.17 = (f32[384,128]{1,0:T(8,128)}, f32[384,128]{1,0:T(8,128)S(1)}, u32[]{:S(2)}, u32[]{:S(2)}) collective-permute-start(f32[384,128]{1,0:T(8,128)} %get-tuple-element.76), channel_id=1, source_target_pairs={{0,18},{2,16},{4,22},{6,20},{8,26},{10,24},{12,30},{14,28},{16,2},... | collective-permute-start | bytes 589832 | tf_op jit(solution)/shard_map/ppermute | solution.py:444
  105.8 10.3 %copy-start.9 = (f32[384,128]{1,0:T(8,128)S(1)}, f32[384,128]{1,0:T(8,128)}, u32[]{:S(2)}) copy-start(f32[384,128]{1,0:T(8,128)} %get-tuple-element.68) | copy-start | bytes 589828
  116.0 1.6 %copy-start.3 = (f32[2,2,384,128]{3,2,1,0:T(8,128)S(1)}, f32[2,2,384,128]{3,2,1,0:T(8,128)}, u32[]{:S(2)}) copy-start(f32[2,2,384,128]{3,2,1,0:T(8,128)} %get-tuple-element.78.stat_ref) | copy-start | bytes 2359300
  116.0 1.6 %copy-start.4 = (bf16[4,64,128]{2,1,0:T(8,128)(2,1)S(1)}, bf16[4,64,128]{2,1,0:T(8,128)(2,1)}, u32[]{:S(2)}) copy-start(bf16[4,64,128]{2,1,0:T(8,128)(2,1)} %get-tuple-element.60.up0) | copy-start | bytes 196612
  116.0 1.6 %copy-start.5 = (s32[4,4]{1,0:T(4,128)S(1)}, s32[4,4]{1,0:T(4,128)}, u32[]{:S(2)}) copy-start(s32[4,4]{1,0:T(4,128)} %pad_add_fusion.info) | copy-start | bytes 196
  116.1 1.5 %collective-permute-start.18 = (f32[384,128]{1,0:T(8,128)S(1)}, f32[384,128]{1,0:T(8,128)S(1)}, u32[]{:S(2)}, u32[]{:S(2)}) collective-permute-start(f32[384,128]{1,0:T(8,128)S(1)} %add_add_fusion.mine_ref), channel_id=1, source_target_pairs={{0,1},{1,0},{2,3},{3,2},{4,5},{5,4},{6,7},{7,6},{8,9},{9,8},{10,11... | collective-permute-start | bytes 589832 | tf_op jit(solution)/shard_map/ppermute | solution.py:538
  117.7 1.9 %copy-start.1 = (f32[2,384,1024]{2,1,0:T(8,128)S(1)}, f32[2,384,1024]{2,1,0:T(8,128)}, u32[]{:S(2)}) copy-start(f32[2,384,1024]{2,1,0:T(8,128)} %get-tuple-element.72.acc_ref) | copy-start | bytes 9437188
  (2 other events, 3.2 us)
